TPU v7x, 256 devices: a whole 4x4x8 slice. The times are simulated.
256 devices in a mesh: orb: 4 (over z_hi, core), space: 64 (over z_lo, y, x).
Axes of the slice: x: 4, y: 4, z: 8 (z_hi: 2, z_lo: 4; z = z_hi * 4 + z_lo), core: 2. Of those that a mesh axis runs over, the one named last changes fastest.
Arguments:
- orbitals: float32 [4, 384, 64, 256], P('orb', 'space'), may hold values from -80 to 80
- atom_type: int32 [384, 64, 256], P('space'), may hold values from 0 to 7
- type_table: float32 [8], replicated, may hold values from -6 to 2
- step_length: float32 [4], replicated, may hold values from 0.1 to 0.4
Outputs:
- new_orbitals: float32 [4, 384, 64, 256], P('orb', 'space')
All inputs are finite; a program needn't handle non-finite values.
Results may differ from a plain program's by a relative error of at most 0.00035.
Values sent between devices are 32-bit elements; how exact they have to be, the bound alone decides.
A program may use at most 128 MiB of HBM per device.

v0:
```python
import jax
import jax.numpy as jnp
from jax import lax
from jax.sharding import PartitionSpec as P

CENTER_TAP = -5369.0 / 1800.0
SIDE_TAPS = (12.0 / 7.0, -15.0 / 56.0, 10.0 / 189.0, -1.0 / 112.0, 2.0 / 1925.0, -1.0 / 16632.0)
SHIFT = 1.0
DAMPING = 0.6
DIAGONAL = SHIFT - 1.5 * CENTER_TAP
HIGH = lax.Precision.HIGHEST


def with_halo(shard, sides, width):
    for axis, dim in sides:
        peers, length = (lax.axis_size(axis), shard.shape[dim])
        up = [(i, (i + 1) % peers) for i in range(peers - 1)]
        down = [(j, i) for i, j in up]
        last = lax.slice_in_dim(shard, length - width, length, axis=dim)
        leading = lax.slice_in_dim(shard, 0, width, axis=dim)
        before = lax.ppermute(last, axis, up)
        after = lax.ppermute(leading, axis, down)
        shard = jnp.concatenate([before, shard, after], axis=dim)
    return shard


def laplacian(field):
    width = field.shape[1]
    padded = with_halo(field, (("space", 1),), 6)
    total = 3.0 * CENTER_TAP * field
    for offset, weight in enumerate(SIDE_TAPS, 1):
        near = (
            padded[:, 6 + offset : 6 + offset + width] + padded[:, 6 - offset : 6 - offset + width]
        )
        near = near + jnp.roll(field, offset, 2) + jnp.roll(field, -offset, 2)
        near = near + jnp.roll(field, offset, 3) + jnp.roll(field, -offset, 3)
        total = total + weight * near
    return total


def smooth(gradient, operator):
    search = DAMPING * gradient / DIAGONAL
    for sweep in range(2):
        search = search + DAMPING * (gradient + 0.5 * operator(search) - SHIFT * search) / DIAGONAL
    return search


def local_potential(atom_type, type_table):
    potential = jnp.zeros(atom_type.shape, jnp.float32)
    for kind in range(type_table.shape[0]):
        potential = potential + jnp.where(atom_type == kind, type_table[kind], jnp.float32(0.0))
    return potential


def inverse_factor(metric):
    lower = jnp.linalg.cholesky(metric)
    inverse = jax.scipy.linalg.solve_triangular(
        lower, jnp.eye(metric.shape[0], dtype=jnp.float32), lower=True
    )
    return inverse.T


def body(orbitals, atom_type, type_table, step_length):
    norb = lax.axis_size("orb")
    position = lax.axis_index("orb")
    selector = (jnp.arange(norb) == position).astype(jnp.float32)
    count = orbitals.shape[1] * orbitals.shape[2] * orbitals.shape[3] * lax.axis_size("space")
    potential = local_potential(atom_type, type_table)
    applied = -0.5 * laplacian(orbitals) + potential[None] * orbitals
    panel = lax.all_gather(orbitals, "orb", axis=0, tiled=True)
    flat_panel = panel.reshape(norb, -1)
    own_flat = orbitals.reshape(1, -1)
    margin_col = jnp.dot(flat_panel, own_flat.T, precision=HIGH)
    projected_col = jnp.dot(flat_panel, applied.reshape(1, -1).T, precision=HIGH)
    margin, projected = lax.psum(
        (margin_col * selector[None, :], projected_col * selector[None, :]), ("orb", "space")
    )
    margin = margin / count
    projected = projected / count
    factor = jnp.linalg.cholesky(margin)
    coupling = jax.scipy.linalg.cho_solve((factor, True), projected)
    column = jnp.dot(coupling, selector, precision=HIGH)
    gradient = applied - jnp.dot(column[None, :], flat_panel, precision=HIGH).reshape(
        orbitals.shape
    )
    search = smooth(gradient, laplacian)
    own_step = jnp.dot(step_length, selector, precision=HIGH)
    moved = orbitals - own_step * search
    moved_panel = lax.all_gather(moved, "orb", axis=0, tiled=True)
    moved_flat = moved_panel.reshape(norb, -1)
    metric_col = jnp.dot(moved_flat, moved.reshape(1, -1).T, precision=HIGH)
    metric = lax.psum(metric_col * selector[None, :], ("orb", "space")) / count
    rotation = inverse_factor(metric)
    weights = jnp.dot(rotation, selector, precision=HIGH)
    return jnp.dot(weights[None, :], moved_flat, precision=HIGH).reshape(orbitals.shape)


def solution(mesh):
    in_specs = (P("orb", "space", None, None), P("space", None, None), P(), P())
    out_specs = P("orb", "space", None, None)
    return jax.shard_map(body, mesh=mesh, in_specs=in_specs, out_specs=out_specs, check_vma=False)
```

profile of v0, /device:TPU:64, one launch (start us, length us, event | category | flops | bytes accessed | tf_op | source)
XLA Modules:
  0.0 326.6 jit_solution(793377490145197080)
XLA Ops:
  6.5 3.5 %collective-permute-start.1 = (f32[1,6,64,256]{3,2,1,0:T(8,128)}, f32[1,6,64,256]{3,2,1,0:T(8,128)S(1)}, u32[]{:S(2)}, u32[]{:S(2)}) collective-permute-start(f32[1,6,64,256]{3,2,1,0:T(8,128)} %param.7), channel_id=1, source_target_pairs={{0,1},{1,2},{2,3},{3,4},{4,5},{5,6},{6,7},{7,8},{8,9},{9,10},{10,1... | collective-permute-start | bytes 1179656 | tf_op jit(solution)/shard_map/ppermute | solution.py:21
  10.1 6.7 %collective-permute-start = (f32[1,6,64,256]{3,2,1,0:T(8,128)}, f32[1,6,64,256]{3,2,1,0:T(8,128)S(1)}, u32[]{:S(2)}, u32[]{:S(2)}) collective-permute-start(f32[1,6,64,256]{3,2,1,0:T(8,128)} %param.7), channel_id=1, source_target_pairs={{1,0},{2,1},{3,2},{4,3},{5,4},{6,5},{7,6},{8,7},{9,8},{10,9},{11,1... | collective-permute-start | bytes 1179656 | tf_op jit(solution)/shard_map/ppermute | solution.py:22
  40.2 9.9 %fusion.106 = f32[1,6,64,256]{3,2,1,0:T(8,128)S(1)} fusion(f32[1,12,64,256]{3,2,1,0:T(8,128)S(1)} %get-tuple-element.154, f32[1,12,64,256]{3,2,1,0:T(8,128)S(1)} %constant_dynamic-update-slice_fusion, f32[1,6,63,256]{3,2,1,0:T(8,128)} %get-tuple-element.150, f32[1,6,1,256]{3,2,1,0:T(1,128)} %get-tuple-element.152, f32[1,6,1,256]{3,2,1,0:T(1,128)} %get-tuple-element.151, ...), kind=kLoop, calls=%fused_computation.149 | loop fusion | flops 9142272 | bytes 15335456 | tf_op jit(solution)/shard_map/add | solution.py:69
  50.6 2.4 copy.23
  53.0 7.3 %convolution_bitcast_fusion.4 = f32[4]{0:T(128)S(1)} fusion(f32[98304,1]{0,1:T(1,128)S(1)} %bitcast.116, f32[4,98304]{1,0:T(4,128)S(1)} %bitcast.106), kind=kOutput, calls=%fused_computation.36 | convolution fusion | flops 4718592 | bytes 1966096 | tf_op jit(solution)/shard_map/dot_general | solution.py:74
  60.3 6.9 %convolution_bitcast_fusion.5 = f32[4]{0:T(128)S(1)} fusion(f32[4,98304]{1,0:T(4,128)S(1)} %bitcast.107, f32[98304,1]{0,1:T(1,128)S(1)} %bitcast.114), kind=kOutput, calls=%fused_computation.37 | convolution fusion | flops 4718592 | bytes 1966096 | tf_op jit(solution)/shard_map/dot_general | solution.py:73
  67.3 75.9 %all-reduce = (f32[4,4]{0,1:T(4,128)S(1)}, f32[4,4]{0,1:T(4,128)S(1)}) all-reduce(f32[4,4]{0,1:T(4,128)S(1)} %get-tuple-element.156, f32[4,4]{0,1:T(4,128)S(1)} %get-tuple-element.155), channel_id=1, replica_groups=mesh['orb'=4,'space'=64] {'orb','space'}, use_global_device_ids=true, to_apply=%region_0.1 | all-reduce | flops 32 | bytes 256 | tf_op jit(solution)/shard_map/psum | solution.py:75
  145.7 2.7 fusion.237
  149.9 5.9 %collective-permute-start.2 = (f32[1,6,64,256]{3,2,1,0:T(8,128)S(1)}, f32[1,6,64,256]{3,2,1,0:T(8,128)S(1)}, u32[]{:S(2)}, u32[]{:S(2)}) collective-permute-start(f32[1,6,64,256]{3,2,1,0:T(8,128)S(1)} %broadcast_multiply_fusion), channel_id=1, source_target_pairs={{1,0},{2,1},{3,2},{4,3},{5,4},{6,5},{7,6},{8,7},{9,8},{10,9},{11,1... | collective-permute-start | bytes 1179656 | tf_op jit(solution)/shard_map/ppermute | solution.py:22
  155.8 1.9 collective-permute-start.3
  158.7 5.4 %collective-permute-done.2 = f32[1,6,64,256]{3,2,1,0:T(8,128)S(1)} collective-permute-done((f32[1,6,64,256]{3,2,1,0:T(8,128)S(1)}, f32[1,6,64,256]{3,2,1,0:T(8,128)S(1)}, u32[]{:S(2)}, u32[]{:S(2)}) %collective-permute-start.2) | collective-permute-done | bytes 393248 | tf_op jit(solution)/shard_map/ppermute | solution.py:22
  164.1 8.3 %collective-permute-done.3 = f32[1,6,64,256]{3,2,1,0:T(8,128)S(1)} collective-permute-done((f32[1,6,64,256]{3,2,1,0:T(8,128)S(1)}, f32[1,6,64,256]{3,2,1,0:T(8,128)S(1)}, u32[]{:S(2)}, u32[]{:S(2)}) %collective-permute-start.3) | collective-permute-done | bytes 393248 | tf_op jit(solution)/shard_map/ppermute | solution.py:21
  172.5 3.2 fusion.57
  177.0 1.9 collective-permute-start.4
  178.9 3.9 %collective-permute-start.5 = (f32[1,6,64,256]{3,2,1,0:T(8,128)S(1)}, f32[1,6,64,256]{3,2,1,0:T(8,128)S(1)}, u32[]{:S(2)}, u32[]{:S(2)}) collective-permute-start(f32[1,6,64,256]{3,2,1,0:T(8,128)S(1)} %fusion.57), channel_id=1, source_target_pairs={{0,1},{1,2},{2,3},{3,4},{4,5},{5,6},{6,7},{7,8},{8,9},{9,10},{10,1... | collective-permute-start | bytes 1179656 | tf_op jit(solution)/shard_map/ppermute | solution.py:21
  183.9 4.7 %collective-permute-done.4 = f32[1,6,64,256]{3,2,1,0:T(8,128)S(1)} collective-permute-done((f32[1,6,64,256]{3,2,1,0:T(8,128)S(1)}, f32[1,6,64,256]{3,2,1,0:T(8,128)S(1)}, u32[]{:S(2)}, u32[]{:S(2)}) %collective-permute-start.4) | collective-permute-done | bytes 393248 | tf_op jit(solution)/shard_map/ppermute | solution.py:22
  188.6 6.1 %collective-permute-done.5 = f32[1,6,64,256]{3,2,1,0:T(8,128)S(1)} collective-permute-done((f32[1,6,64,256]{3,2,1,0:T(8,128)S(1)}, f32[1,6,64,256]{3,2,1,0:T(8,128)S(1)}, u32[]{:S(2)}, u32[]{:S(2)}) %collective-permute-start.5) | collective-permute-done | bytes 393248 | tf_op jit(solution)/shard_map/ppermute | solution.py:21
  194.7 5.0 %multiply_subtract_fusion = f32[1,6,64,256]{3,2,1,0:T(8,128)} fusion(f32[1,6,64,256]{3,2,1,0:T(8,128)S(1)} %copy-done, f32[1,6,64,256]{3,2,1,0:T(8,128)S(1)} %fusion.57, f32[1,6,64,6]{3,2,1,0:T(8,128)S(1)} %get-tuple-element.54, f32[1,6,64,250]{3,2,1,0:T(8,128)S(1)} %get-tuple-element.56, f32[1,6,64,250]{3,2,1,0:T(8,128)S(1)} %get-tuple-element.55, ...), kind=kLoop, calls=%fused_computation.195 | loop fusion | flops 8355840 | bytes 12189700 | tf_op jit(solution)/shard_map/sub | solution.py:88
  199.7 1.4 copy.27
  201.1 27.2 %all-gather.5.cloned.1.call-done = f32[4,6,64,256]{3,2,1,0:T(8,128)} async-done(((f32[1,6,64,256]{3,2,1,0:T(8,128)}), f32[4,6,64,256]{3,2,1,0:T(8,128)}) %all-gather.5.cloned.1.call-update) | async-done | bytes 1572880 | tf_op jit(solution)/shard_map/all_gather | solution.py:89
  228.3 2.4 copy.26
  230.8 6.9 %convolution_bitcast_fusion.3 = f32[4]{0:T(128)S(1)} fusion(f32[4,98304]{1,0:T(4,128)S(1)} %bitcast.109, f32[98304,1]{0,1:T(1,128)S(1)} %bitcast.115), kind=kOutput, calls=%fused_computation.35 | convolution fusion | flops 4718592 | bytes 1966096 | tf_op jit(solution)/shard_map/dot_general | solution.py:91
  237.7 76.1 %psum.23 = f32[4,4]{0,1:T(4,128)S(1)} all-reduce(f32[4,4]{0,1:T(4,128)S(1)} %broadcast_multiply_fusion.1), channel_id=1, replica_groups=mesh['orb'=4,'space'=64] {'orb','space'}, use_global_device_ids=true, to_apply=%region_4.7 | all-reduce | flops 16 | bytes 128 | tf_op jit(solution)/shard_map/psum | solution.py:92
  316.3 2.7 fusion.238
  (146 shorter events, 34.2 us)
Async XLA Ops:
  6.5 11.6 %copy-start = (f32[1,6,64,256]{3,2,1,0:T(8,128)S(1)}, f32[1,6,64,256]{3,2,1,0:T(8,128)}, u32[]{:S(2)}) copy-start(f32[1,6,64,256]{3,2,1,0:T(8,128)} %param.7) | copy-start | bytes 1179652
  6.5 44.0 %all-gather.3.cloned.1.call-start = ((), (), s32[]{:S(2)}) async-start(), calls=%async_computation | async-start | bytes 1966080 | tf_op jit(solution)/shard_map/all_gather | solution.py:70
  6.5 32.7 %collective-permute-start.1 = (f32[1,6,64,256]{3,2,1,0:T(8,128)}, f32[1,6,64,256]{3,2,1,0:T(8,128)S(1)}, u32[]{:S(2)}, u32[]{:S(2)}) collective-permute-start(f32[1,6,64,256]{3,2,1,0:T(8,128)} %param.7), channel_id=1, source_target_pairs={{0,1},{1,2},{2,3},{3,4},{4,5},{5,6},{6,7},{7,8},{8,9},{9,10},{10,1... | collective-permute-start | bytes 1179656 | tf_op jit(solution)/shard_map/ppermute | solution.py:21
  10.1 29.3 %collective-permute-start = (f32[1,6,64,256]{3,2,1,0:T(8,128)}, f32[1,6,64,256]{3,2,1,0:T(8,128)S(1)}, u32[]{:S(2)}, u32[]{:S(2)}) collective-permute-start(f32[1,6,64,256]{3,2,1,0:T(8,128)} %param.7), channel_id=1, source_target_pairs={{1,0},{2,1},{3,2},{4,3},{5,4},{6,5},{7,6},{8,7},{9,8},{10,9},{11,1... | collective-permute-start | bytes 1179656 | tf_op jit(solution)/shard_map/ppermute | solution.py:22
  16.8 211.6 %all-gather.5.cloned.1.call-start = ((), (), s32[]{:S(2)}) async-start(), calls=%async_computation.1 | async-start | bytes 1966080 | tf_op jit(solution)/shard_map/all_gather | solution.py:89
  34.0 2.6 copy-start.16
  35.1 3.4 %copy-start.15 = (f32[8]{0:T(128)S(1)}, f32[8]{0:T(128)}, u32[]{:S(2)}) copy-start(f32[8]{0:T(128)} %param.9) | copy-start | bytes 100
  37.3 2.1 copy-start.8
  37.3 2.1 copy-start.9
  38.5 1.1 copy-start.2
  38.5 1.3 copy-start.3
  38.5 1.4 copy-start.4
  38.5 1.5 copy-start.5
  38.5 1.6 copy-start.6
  38.5 1.7 copy-start.7
  38.5 1.7 copy-start.11
  38.5 1.7 copy-start.12
  38.6 1.7 copy-start.13
  38.6 1.7 copy-start.14
  53.0 7.3 %copy-start.10 = (f32[1,1,384,256]{3,1,2,0:T(1,128)S(1)}, f32[1,1,384,256]{3,1,2,0:T(1,128)}, u32[]{:S(2)}) copy-start(f32[1,1,384,256]{3,1,2,0:T(1,128)} %copy.24) | copy-start | bytes 1179652
  149.9 14.3 %collective-permute-start.2 = (f32[1,6,64,256]{3,2,1,0:T(8,128)S(1)}, f32[1,6,64,256]{3,2,1,0:T(8,128)S(1)}, u32[]{:S(2)}, u32[]{:S(2)}) collective-permute-start(f32[1,6,64,256]{3,2,1,0:T(8,128)S(1)} %broadcast_multiply_fusion), channel_id=1, source_target_pairs={{1,0},{2,1},{3,2},{4,3},{5,4},{6,5},{7,6},{8,7},{9,8},{10,9},{11,1... | collective-permute-start | bytes 1179656 | tf_op jit(solution)/shard_map/ppermute | solution.py:22
  155.8 16.7 %collective-permute-start.3 = (f32[1,6,64,256]{3,2,1,0:T(8,128)S(1)}, f32[1,6,64,256]{3,2,1,0:T(8,128)S(1)}, u32[]{:S(2)}, u32[]{:S(2)}) collective-permute-start(f32[1,6,64,256]{3,2,1,0:T(8,128)S(1)} %broadcast_multiply_fusion), channel_id=1, source_target_pairs={{0,1},{1,2},{2,3},{3,4},{4,5},{5,6},{6,7},{7,8},{8,9},{9,10},{10,1... | collective-permute-start | bytes 1179656 | tf_op jit(solution)/shard_map/ppermute | solution.py:21
  177.0 11.5 %collective-permute-start.4 = (f32[1,6,64,256]{3,2,1,0:T(8,128)S(1)}, f32[1,6,64,256]{3,2,1,0:T(8,128)S(1)}, u32[]{:S(2)}, u32[]{:S(2)}) collective-permute-start(f32[1,6,64,256]{3,2,1,0:T(8,128)S(1)} %fusion.57), channel_id=1, source_target_pairs={{1,0},{2,1},{3,2},{4,3},{5,4},{6,5},{7,6},{8,7},{9,8},{10,9},{11,1... | collective-permute-start | bytes 1179656 | tf_op jit(solution)/shard_map/ppermute | solution.py:22
  178.9 15.8 %collective-permute-start.5 = (f32[1,6,64,256]{3,2,1,0:T(8,128)S(1)}, f32[1,6,64,256]{3,2,1,0:T(8,128)S(1)}, u32[]{:S(2)}, u32[]{:S(2)}) collective-permute-start(f32[1,6,64,256]{3,2,1,0:T(8,128)S(1)} %fusion.57), channel_id=1, source_target_pairs={{0,1},{1,2},{2,3},{3,4},{4,5},{5,6},{6,7},{7,8},{8,9},{9,10},{10,1... | collective-permute-start | bytes 1179656 | tf_op jit(solution)/shard_map/ppermute | solution.py:21
  (1 other events, 1.0 us)
Sparse Core Ops, SparseCore 0:
  16.9 33.2 all-gather.2
  199.9 28.4 all-gather.4
where the time goes:
time: 331 us; the launch traced here: 327 us
  blocking collectives  152 us (46%)
  waiting for transfers between devices  51.8 us (16%)
  local copies, waits for them, and re-layouts  34.6 us (10%)
  matrix products  27.3 us (8%)
  starting transfers between devices  23.9 us (7%)
  other arithmetic  23.1 us (7%)
  between operations  13.9 us (4%)
    psum x1, blocking collectives, body(): metric = lax.psum(metric_col * selector[None, :], ('orb', 'space')) / count  76.1 us
    psum x1, blocking collectives, body(): lax.psum((margin_col * selector[None, :], projected_col * selector[None,...  75.9 us
    all_gather x1, waiting for transfers between devices, body(): moved_panel = lax.all_gather(moved, 'orb', axis=0, tiled=True)  27.2 us
    slice x36, local copies, waits for them, and re-layouts, laplacian(): near = near + jnp.roll(field, offset, 3) + jnp.roll(field, -offset, 3)  14.6 us
    ppermute x3, waiting for transfers between devices, with_halo(): before = lax.ppermute(last, axis, up)  14.5 us
    ppermute x3, starting transfers between devices, with_halo(): after = lax.ppermute(leading, axis, down)  14.5 us
    ppermute x3, waiting for transfers between devices, with_halo(): after = lax.ppermute(leading, axis, down)  10.1 us
    add x1, other arithmetic, body(): applied = -0.5 * laplacian(orbitals) + potential[None] * orbitals  9.89 us
  transfers between devices with their start and end apart: 8, of which 5 were waited for; matrix products, arithmetic and copies ran while one was open for 11% of the time, Pallas kernels for 0%

commit v1 on v0

v1 whole, which is shorter than its diff:
```python
import jax
import jax.numpy as jnp
import numpy as np
from jax import lax
from jax.experimental import pallas as pl
from jax.experimental.pallas import tpu as pltpu
from jax.sharding import PartitionSpec as P

MESH = pl.DeviceIdType.MESH
HIGH = lax.Precision.HIGHEST
CENTER_TAP = -5369.0 / 1800.0
SIDE_TAPS = (12.0 / 7.0, -15.0 / 56.0, 10.0 / 189.0, -1.0 / 112.0, 2.0 / 1925.0, -1.0 / 16632.0)
SHIFT = 1.0
DAMPING = 0.6
DIAGONAL = SHIFT - 1.5 * CENTER_TAP
CELLS = 384 * 64 * 256
NORB = 4
NTYPES = 8

SIDE = tuple(-0.5 * w for w in SIDE_TAPS)
CENTER = -1.5 * CENTER_TAP
W = DAMPING / DIAGONAL
P1, P2, P3 = 3.0 * W, -3.0 * W * W, W * W * W

PL, RW, CO = 12, 16, 128
H = 6
PAIRS = [(i, j) for i in range(NORB) for j in range(i + 1)]


def z_tables():
    own = np.zeros((CO, CO), np.float32)
    for a in range(CO):
        for b in range(CO):
            d = abs(a - b)
            if d == 0:
                own[a, b] = CENTER
            elif d <= H:
                own[a, b] = SIDE[d - 1]
    pick = np.zeros((16, CO), np.float32)
    spread = np.zeros((16, CO), np.float32)
    for i in range(H):
        pick[i, CO - H + i] = 1.0
        pick[H + i, i] = 1.0
        for b in range(CO):
            d = b + H - i
            if 1 <= d <= H:
                spread[i, b] = SIDE[d - 1]
            d = CO + i - b
            if 1 <= d <= H:
                spread[H + i, b] = SIDE[d - 1]
    return own, pick, spread


def dot(a, b, ca, cb):
    return lax.dot_general(
        a, b, (((ca,), (cb,)), ((), ())), precision=HIGH, preferred_element_type=jnp.float32
    )


def cholesky(s):
    low = {}
    inv = []
    for i in range(NORB):
        for j in range(i):
            t = s[i, j]
            for k in range(j):
                t = t - low[i, k] * low[j, k]
            low[i, j] = t * inv[j]
        t = s[i, i]
        for k in range(i):
            t = t - low[i, k] * low[i, k]
        root = jnp.sqrt(t)
        low[i, i] = root
        inv.append(1.0 / root)
    return low, inv


def kernel(
    x_ref, type_ref, own_ref, pick_ref, spread_ref, table_ref, step_ref, out_ref,
    xf, wf, gf, vs, vf, mx, mw, base, new, zz, zs, zr, gram, coef, ra, rb,
    t_send, t_recv, v_send, v_recv, h_send, h_recv, b_send, b_recv, r_send, r_recv,
):
    s = lax.axis_index("space")
    o = lax.axis_index("orb")
    h, c, q, x = o // 2, o % 2, s // 4, s % 4
    mine = c == x // 2
    link = 2 * q + c
    has_left, has_right = link > 0, link < 31

    def device(hh, cc, qq, xx):
        return (2 * hh + cc, 4 * qq + xx)

    left = device(h, (link + 31) % 2, ((link + 31) % 32) // 2, x)
    right = device(h, (link + 1) % 2, ((link + 1) % 32) // 2, x)
    up = device(h, c, q, (x + 3) % 4)
    down = device(h, c, q, (x + 1) % 4)
    across = device(1 - h, c, q, x)

    me1 = (x * 2 + h) * 2 + c
    me2 = q

    def peer1(k):
        i = (me1 + k) % 16
        return device((i // 2) % 2, i % 2, q, i // 4)

    def peer2(k):
        return device(h, c, (me2 + k) % 16, x)

    barrier = pltpu.get_barrier_semaphore()

    def hello(k, carry):
        pl.semaphore_signal(barrier, inc=1, device_id=peer1(k), device_id_type=MESH)
        pl.semaphore_signal(barrier, inc=1, device_id=peer2(k), device_id_type=MESH)
        return carry

    lax.fori_loop(1, 16, hello, 0)

    @pl.when(jnp.logical_and(c == 0, has_left))
    def _():
        pl.semaphore_signal(barrier, inc=1, device_id=left, device_id_type=MESH)

    @pl.when(jnp.logical_and(c == 1, has_right))
    def _():
        pl.semaphore_signal(barrier, inc=1, device_id=right, device_id_type=MESH)

    kinds = type_ref[...]
    potential = jnp.zeros(kinds.shape, jnp.float32)
    for kind in range(NTYPES):
        potential = jnp.where(kinds == kind, table_ref[kind], potential)
    vs[...] = potential

    for f in (xf, wf, gf):
        @pl.when(jnp.logical_not(has_left))
        def _():
            f[:, 0:H] = jnp.zeros((NORB, H, RW + 16, CO), jnp.float32)

        @pl.when(jnp.logical_not(has_right))
        def _():
            f[:, H + PL:] = jnp.zeros((NORB, H, RW + 16, CO), jnp.float32)
    gram[...] = jnp.zeros(gram.shape, jnp.float32)

    @pl.when(jnp.logical_or(jnp.logical_and(c == 0, has_left), jnp.logical_and(c == 1, has_right)))
    def _():
        pl.semaphore_wait(barrier, 31)

    @pl.when(jnp.logical_not(jnp.logical_or(jnp.logical_and(c == 0, has_left), jnp.logical_and(c == 1, has_right))))
    def _():
        pl.semaphore_wait(barrier, 30)

    def rows_of(xx):
        return pl.ds(pl.multiple_of(16 * xx, 16), 16)

    def cols_of(hh):
        return pl.ds(pl.multiple_of(CO * hh, CO), CO)

    def part(ref, xx, hh):
        return ref.at[:, rows_of(xx), cols_of(hh)]

    half = x % 2

    def scatter(j, k):
        hh, xx = (h + j) % 2, (x + k) % 4
        n = 4 * j + k
        return part(x_ref, xx, hh), xf.at[o, pl.ds(H + 6 * half, 6), pl.ds(8, 16)], t_send.at[n], t_recv.at[2 * o + half], device(hh, x // 2, q, xx)

    def remote(src, dst, ss, rs, dev):
        return pltpu.make_async_remote_copy(
            src_ref=src, dst_ref=dst, send_sem=ss, recv_sem=rs, device_id=dev, device_id_type=MESH
        )

    for j in (1, 0):
        for k in (2, 1, 3, 0):
            a = scatter(j, k)
            if j == 0 and k == 0:
                @pl.when(mine)
                def _():
                    pltpu.make_async_copy(a[0], a[1], a[3]).start()

                @pl.when(jnp.logical_not(mine))
                def _():
                    remote(*a).start()
            else:
                remote(*a).start()

    def spread_v(k, n):
        xx = (x + k) % 4
        return part(vs, xx, h), vf.at[pl.ds(6 * half, 6)], v_send.at[n], v_recv.at[half], device(h, x // 2, q, xx)

    @pl.when(mine)
    def _():
        a = spread_v(0, 0)
        pltpu.make_async_copy(a[0], a[1], a[3]).start()
        remote(*spread_v(2, 1)).start()

    @pl.when(jnp.logical_not(mine))
    def _():
        remote(*spread_v(1, 0)).start()
        remote(*spread_v(3, 1)).start()

    own = (slice(H, H + PL), slice(8, 8 + RW))

    def halo_copies(f, r):
        full = slice(None)
        return (
            (has_left, remote(f.at[:, H:2 * H, 8:8 + RW], f.at[:, H + PL:, 8:8 + RW], h_send.at[5 * r], h_recv.at[5 * r + 1], left)),
            (has_right, remote(f.at[:, PL:PL + H, 8:8 + RW], f.at[:, 0:H, 8:8 + RW], h_send.at[5 * r + 1], h_recv.at[5 * r], right)),
            (None, remote(f.at[:, H:H + PL, 8:16], f.at[:, H:H + PL, 24:32], h_send.at[5 * r + 2], h_recv.at[5 * r + 3], up)),
            (None, remote(f.at[:, H:H + PL, 16:24], f.at[:, H:H + PL, 0:8], h_send.at[5 * r + 3], h_recv.at[5 * r + 2], down)),
            (None, remote(zs.at[r], zr.at[r], h_send.at[5 * r + 4], h_recv.at[5 * r + 4], across)),
        )

    def guarded(cond, fn):
        if cond is None:
            fn()
        else:
            pl.when(cond)(fn)

    def share(f):
        return f[:, own[0], own[1]].reshape(NORB * PL * RW, CO)

    def halo_start(f, r):
        copies = halo_copies(f, r)
        flat = share(f)
        zs[r] = dot(pick_ref[...], flat, 1, 1)
        for cond, cp in (copies[4],) + copies[:4]:
            guarded(cond, cp.start)
        zz[...] = dot(flat, own_ref[...], 1, 0)

    def halo_finish(f, r):
        copies = halo_copies(f, r)
        for cond, cp in copies:
            guarded(cond, cp.wait_send)
        guarded(has_left, copies[1][1].wait_recv)
        guarded(has_right, copies[0][1].wait_recv)
        for _, cp in copies[2:]:
            cp.wait_recv()
        zz[...] += dot(zr[r], spread_ref[...], 0, 0)

    def kinetic(f, i, p):
        at = pl.ds(pl.multiple_of((i * PL + p) * RW, RW), RW)
        total = zz[at]
        for n in range(1, H + 1):
            near = f[i, p + H + n, 8:8 + RW] + f[i, p + H - n, 8:8 + RW]
            near = near + f[i, p + H, 8 + n:8 + RW + n] + f[i, p + H, 8 - n:8 + RW - n]
            total = total + SIDE[n - 1] * near
        return total

    def each(fn):
        def step(n, carry):
            fn(n // PL, n % PL)
            return carry
        lax.fori_loop(0, NORB * PL, step, 0)

    def each_plane(fn):
        def step(p, carry):
            fn(p)
            return carry
        lax.fori_loop(0, PL, step, 0)

    def reduce_start(v, buf, send, recv, me, peer):
        buf[me] = v

        def go(k, carry):
            remote(buf.at[me], buf.at[me], send, recv, peer(k)).start()
            return carry

        lax.fori_loop(1, 16, go, 0)

    def reduce_finish(buf, send, recv, peer):
        cp = remote(buf.at[pl.ds(0, 15)], buf.at[pl.ds(0, 15)], send, recv, peer(1))
        cp.wait_send()
        cp.wait_recv()
        return jnp.sum(buf[...], axis=0)

    def local_sums(rows):
        for n, v in enumerate(rows):
            gram[n:n + 1] = jnp.sum(v, axis=0, keepdims=True)
        return dot(jnp.ones((8, CO), jnp.float32), gram[...], 1, 1)[0:1]

    def spread_out(v, n):
        return jnp.broadcast_to(v[:, n:n + 1], (8, CO)) * (1.0 / CELLS)

    def planes(f, i, p, halo=True):
        v = f[i, p + H, 8:8 + RW] if halo else f[i, p]
        return v.reshape(2, 8, CO)

    for i in range(NORB):
        for p in range(2):
            cp = remote(xf.at[i, pl.ds(H + 6 * p, 6), pl.ds(8, 16)], xf.at[i, pl.ds(H + 6 * p, 6), pl.ds(8, 16)], t_send.at[0], t_recv.at[2 * i + p], across)
            cp.wait_recv()
    halo_start(xf, 0)
    for p in range(2):
        remote(vf.at[pl.ds(6 * p, 6)], vf.at[pl.ds(6 * p, 6)], v_send.at[0], v_recv.at[p], across).wait_recv()
    halo_finish(xf, 0)

    def first(i, p):
        kx = kinetic(xf, i, p)
        v = xf[i, p + H, 8:8 + RW]
        wf[i, p + H, 8:8 + RW] = kx + vf[p] * v
        mx[i, p] = kx + SHIFT * v

    each(first)
    halo_start(wf, 1)

    def products(p, acc):
        xs = [planes(xf, i, p) for i in range(NORB)]
        ws = [planes(wf, i, p) for i in range(NORB)]
        acc = list(acc)
        for n, (i, j) in enumerate(PAIRS):
            acc[n] = acc[n] + jnp.sum(xs[i] * xs[j], axis=0)
        for j in range(NORB):
            for i in range(NORB):
                n = 10 + 4 * j + i
                acc[n] = acc[n] + jnp.sum(xs[j] * ws[i], axis=0)
        return tuple(acc)

    zero = jnp.zeros((8, CO), jnp.float32)
    acc = lax.fori_loop(0, PL, products, (zero,) * 26)
    reduce_start(local_sums(acc), ra.at[0], r_send.at[0], r_recv.at[0], me1, peer1)
    v = reduce_finish(ra.at[0], r_send.at[0], r_recv.at[0], peer1)
    reduce_start(v, rb.at[0], r_send.at[1], r_recv.at[1], me2, peer2)
    halo_finish(wf, 1)

    def second(i, p):
        mw[i, p] = kinetic(wf, i, p) + SHIFT * wf[i, p + H, 8:8 + RW]

    each(second)
    v = reduce_finish(rb.at[0], r_send.at[1], r_recv.at[1], peer2)
    margin = {(i, j): spread_out(v, n) for n, (i, j) in enumerate(PAIRS)}
    low, inv = cholesky(margin)
    for i in range(NORB):
        y = []
        for j in range(NORB):
            t = spread_out(v, 10 + 4 * j + i)
            for k in range(j):
                t = t - low[j, k] * y[k]
            y.append(t * inv[j])
        for j in reversed(range(NORB)):
            t = y[j]
            for k in range(j + 1, NORB):
                t = t - low[k, j] * y[k]
            y[j] = t * inv[j]
            coef[4 * i + j] = y[j]

    def couple(p):
        ms = [planes(mx, j, p, False) for j in range(NORB)]
        for i in range(NORB):
            t = planes(mw, i, p, False)
            for j in range(NORB):
                t = t - coef[4 * i + j] * ms[j]
            gf[i, p + H, 8:8 + RW] = t.reshape(RW, CO)

    each_plane(couple)
    halo_start(gf, 2)

    def prepare(p):
        xs = [planes(xf, j, p) for j in range(NORB)]
        for i in range(NORB):
            t = planes(wf, i, p)
            for j in range(NORB):
                t = t - coef[4 * i + j] * xs[j]
            t = P1 * t + (P2 + SHIFT * P3) * planes(gf, i, p)
            base[i, p] = (xs[i] - step_ref[i] * t).reshape(RW, CO)

    each_plane(prepare)
    halo_finish(gf, 2)

    def third(i, p):
        base[i, p] = base[i, p] - (P3 * step_ref[i]) * kinetic(gf, i, p)

    each(third)

    def metric(p, acc):
        ms = [planes(base, i, p, False) for i in range(NORB)]
        return tuple(a + jnp.sum(ms[i] * ms[j], axis=0) for a, (i, j) in zip(acc, PAIRS))

    acc = lax.fori_loop(0, PL, metric, (zero,) * 10)
    reduce_start(local_sums(acc), ra.at[1], r_send.at[2], r_recv.at[2], me1, peer1)
    v = reduce_finish(ra.at[1], r_send.at[2], r_recv.at[2], peer1)
    reduce_start(v, rb.at[1], r_send.at[3], r_recv.at[3], me2, peer2)
    v = reduce_finish(rb.at[1], r_send.at[3], r_recv.at[3], peer2)
    low, inv = cholesky({(i, j): spread_out(v, n) for n, (i, j) in enumerate(PAIRS)})
    lowinv = {}
    for j in range(NORB):
        lowinv[j, j] = inv[j]
        for i in range(j + 1, NORB):
            t = low[i, j] * lowinv[j, j]
            for k in range(j + 1, i):
                t = t + low[i, k] * lowinv[k, j]
            lowinv[i, j] = -t * inv[i]
    for n, ij in enumerate(PAIRS):
        coef[n] = lowinv[ij]

    def rotate(p):
        ms = [planes(base, j, p, False) for j in range(NORB)]
        for i in range(NORB):
            t = None
            for n, (a, j) in enumerate(PAIRS):
                if a == i:
                    term = coef[n] * ms[j]
                    t = term if t is None else t + term
            new[i, p] = t.reshape(RW, CO)

    each_plane(rotate)

    def back(j, i, m):
        hh, cc, pp = (h + j) % 2, (c + i) % 2, (x + m) % 2
        return new.at[2 * hh + cc, pl.ds(6 * pp, 6)], part(out_ref, x, h), b_send.at[4 * j + 2 * i + m], b_recv.at[2 * x + h], device(hh, cc, q, 2 * c + pp)

    order = [(j, i, m) for j in (1, 0) for i in (1, 0) for m in (1, 0)]
    for jim in order:
        a = back(*jim)
        if jim == (0, 0, 0):
            @pl.when(mine)
            def _():
                pltpu.make_async_copy(a[0], a[1], a[3]).start()

            @pl.when(jnp.logical_not(mine))
            def _():
                remote(*a).start()
        else:
            remote(*a).start()

    for j in (1, 0):
        for k in (2, 1, 3, 0):
            a = scatter(j, k)
            if j == 0 and k == 0:
                @pl.when(jnp.logical_not(mine))
                def _():
                    remote(*a).wait_send()
            else:
                remote(*a).wait_send()

    @pl.when(mine)
    def _():
        remote(*spread_v(2, 1)).wait_send()

    @pl.when(jnp.logical_not(mine))
    def _():
        remote(*spread_v(1, 0)).wait_send()
        remote(*spread_v(3, 1)).wait_send()

    for jim in order:
        a = back(*jim)
        if jim == (0, 0, 0):
            @pl.when(jnp.logical_not(mine))
            def _():
                remote(*a).wait_send()
        else:
            remote(*a).wait_send()
    for xx in range(4):
        for hh in range(2):
            dst = out_ref.at[:, pl.ds(16 * xx, 16), pl.ds(CO * hh, CO)]
            remote(dst, dst, b_send.at[0], b_recv.at[2 * xx + hh], across).wait_recv()


def body(orbitals, atom_type, type_table, step_length):
    shape = orbitals.shape
    own, pick, spread = z_tables()
    vmem = pl.BlockSpec(memory_space=pltpu.VMEM)
    smem = pl.BlockSpec(memory_space=pltpu.SMEM)
    f32 = jnp.float32
    share = (NORB, PL, RW, CO)
    wide = (NORB, PL + 2 * H, RW + 16, CO)
    rows = NORB * PL * RW
    dma = pltpu.SemaphoreType.DMA
    out = pl.pallas_call(
        kernel,
        out_shape=jax.ShapeDtypeStruct(shape[1:], f32),
        in_specs=[vmem] * 5 + [smem] * 2,
        out_specs=vmem,
        scratch_shapes=[
            pltpu.VMEM(wide, f32), pltpu.VMEM(wide, f32), pltpu.VMEM(wide, f32),
            pltpu.VMEM(shape[1:], f32), pltpu.VMEM((PL, RW, CO), f32),
            pltpu.VMEM(share, f32), pltpu.VMEM(share, f32), pltpu.VMEM(share, f32), pltpu.VMEM(share, f32),
            pltpu.VMEM((rows, CO), f32),
            pltpu.VMEM((3, 16, rows), f32), pltpu.VMEM((3, 16, rows), f32),
            pltpu.VMEM((CO, CO), f32), pltpu.VMEM((16, 8, CO), f32),
            pltpu.VMEM((2, 16, 1, CO), f32), pltpu.VMEM((2, 16, 1, CO), f32),
            dma((8,)), dma((8,)), dma((2,)), dma((2,)), dma((15,)), dma((15,)),
            dma((8,)), dma((8,)), dma((4,)), dma((4,)),
        ],
        compiler_params=pltpu.CompilerParams(
            collective_id=0, has_side_effects=True, vmem_limit_bytes=40 << 20
        ),
        name="step",
    )(orbitals.reshape(shape[1:]), atom_type, own, pick, spread, type_table, step_length)
    return out.reshape(shape)


def solution(mesh):
    in_specs = (P("orb", "space", None, None), P("space", None, None), P(), P())
    out_specs = P("orb", "space", None, None)
    return jax.shard_map(body, mesh=mesh, in_specs=in_specs, out_specs=out_specs, check_vma=False)
```

time: 331 us -> 84 us (0.25); the launches traced: 327 us -> 83.7 us
  blocking collectives: 152 us -> 0 us
  Pallas kernels: 0 us -> 78.1 us
  waiting for transfers between devices: 51.8 us -> 0 us
  local copies, waits for them, and re-layouts: 34.6 us -> 5.64 us
  matrix products: 27.3 us -> 0 us
  starting transfers between devices: 23.9 us -> 0 us
  other arithmetic: 23.1 us -> 0 us
  between operations: 13.9 us -> 0.02 us
    psum x2 -> x0, blocking collectives: 152 us -> none  [the longest x1 76.1 us: body(): metric = lax.psum(metric_col * selector[None, :], ('orb', 'space')) / count]
    pallas_call x0 -> x1, Pallas kernels: none -> 78.1 us  [body(): pl.pallas_call(kernel, out_shape=jax.ShapeDtypeStruct(shape[1:], f32), in...]
    all_gather x2 -> x0, waiting for transfers between devices: 27.2 us -> none  [the longest x1 27.2 us: body(): moved_panel = lax.all_gather(moved, 'orb', axis=0, tiled=True)]
    dot_general x7 -> x0, matrix products: 26.7 us -> none  [the longest x1 7.27 us: body(): jnp.dot(flat_panel, applied.reshape(1, -1).T, precision=HIGH)]
    slice x73 -> x0, local copies, waits for them, and re-layouts: 24.9 us -> none  [the longest x36 14.6 us: laplacian(): near = near + jnp.roll(field, offset, 3) + jnp.roll(field, -offset, 3)]
    ppermute x6 -> x0, waiting for transfers between devices: 24.6 us -> none  [the longest x3 14.5 us: with_halo(): before = lax.ppermute(last, axis, up)]
    ppermute x6 -> x0, starting transfers between devices: 23.8 us -> none  [the longest x3 14.5 us: with_halo(): after = lax.ppermute(leading, axis, down)]
    add x2 -> x0, other arithmetic: 13.1 us -> none  [the longest x1 9.89 us: body(): applied = -0.5 * laplacian(orbitals) + potential[None] * orbitals]
  transfers between devices with their start and end apart: 8 -> 0, of which waited for: 5 -> 0; matrix products, arithmetic and copies ran while one was open for 11% -> 0% of each run, Pallas kernels for 0% -> 0%
where the time goes in v1:
time: 84 us; the launch traced here: 83.7 us
  Pallas kernels  78.1 us (93%)
  local copies, waits for them, and re-layouts  5.64 us (7%)
    pallas_call x1, Pallas kernels, body(): pl.pallas_call(kernel, out_shape=jax.ShapeDtypeStruct(shape[1:], f32), in...  78.1 us
    unnamed x15, local copies, waits for them, and re-layouts  5.64 us

profile of v1, /device:TPU:64, one launch (start us, length us, event | category | flops | bytes accessed | tf_op | source)
XLA Modules:
  0.0 83.7 jit_solution(9342780757690697050)
XLA Ops:
  0.0 0.0 copy-start.6
  0.0 0.0 copy-start.5
  0.0 0.7 copy-done.6
  0.7 0.0 copy-done.5
  0.7 0.0 copy-start
  0.7 1.0 %copy-done = f32[1,6,64,256]{3,2,1,0:T(8,128)S(1)} copy-done((f32[1,6,64,256]{3,2,1,0:T(8,128)S(1)}, f32[1,6,64,256]{3,2,1,0:T(8,128)}, u32[]{:S(2)}) %copy-start) | copy-done | bytes 393240
  1.7 0.0 copy-start.1
  1.7 1.0 %copy-done.1 = s32[6,64,256]{2,1,0:T(8,128)S(1)} copy-done((s32[6,64,256]{2,1,0:T(8,128)S(1)}, s32[6,64,256]{2,1,0:T(8,128)}, u32[]{:S(2)}) %copy-start.1) | copy-done | bytes 393240
  2.7 0.0 copy-start.2
  2.7 0.8 copy-done.2
  3.5 0.0 copy-start.3
  3.5 0.7 copy-done.3
  4.2 0.0 copy-start.4
  4.2 0.7 copy-done.4
  4.9 78.1 %step.1 = f32[6,64,256]{2,1,0:T(8,128)S(1)} custom-call(f32[6,64,256]{2,1,0:T(8,128)S(1)} %bitcast.3, s32[6,64,256]{2,1,0:T(8,128)S(1)} %copy-done.1, f32[128,128]{1,0:T(8,128)S(1)} %copy-done.2, f32[16,128]{1,0:T(8,128)S(1)} %copy-done.4, f32[16,128]{1,0:T(8,128)S(1)} %copy-done.3, f32[8]{0:T(128)S(1)} %copy-done.5, f32[4]{0:T(128)S(1)} %copy-done.6), custom_call_target="tpu_custom_call" | custom-call | tf_op jit(solution)/shard_map/step/pallas_call | solution.py:467
  83.0 0.7 copy.9
Async XLA Ops:
  0.0 0.7 copy-start.6
  0.0 0.7 copy-start.5
  0.7 1.0 %copy-start = (f32[1,6,64,256]{3,2,1,0:T(8,128)S(1)}, f32[1,6,64,256]{3,2,1,0:T(8,128)}, u32[]{:S(2)}) copy-start(f32[1,6,64,256]{3,2,1,0:T(8,128)} %param.7) | copy-start | bytes 1179652
  1.7 1.0 %copy-start.1 = (s32[6,64,256]{2,1,0:T(8,128)S(1)}, s32[6,64,256]{2,1,0:T(8,128)}, u32[]{:S(2)}) copy-start(s32[6,64,256]{2,1,0:T(8,128)} %type_ref.1) | copy-start | bytes 1179652
  2.7 0.8 %copy-start.2 = (f32[128,128]{1,0:T(8,128)S(1)}, f32[128,128]{1,0:T(8,128)}, u32[]{:S(2)}) copy-start(f32[128,128]{1,0:T(8,128)} %constant.6.clone.own_ref) | copy-start | bytes 196612
  3.5 0.7 copy-start.3
  4.2 0.7 copy-start.4

commit v2 on v1

v2 whole, which is shorter than its diff:
```python
import jax
import jax.numpy as jnp
from jax import lax
from jax.experimental import pallas as pl
from jax.experimental.pallas import tpu as pltpu
from jax.sharding import PartitionSpec as P

MESH = pl.DeviceIdType.MESH
HIGH = lax.Precision.HIGHEST
CENTER_TAP = -5369.0 / 1800.0
SIDE_TAPS = (12.0 / 7.0, -15.0 / 56.0, 10.0 / 189.0, -1.0 / 112.0, 2.0 / 1925.0, -1.0 / 16632.0)
SHIFT = 1.0
DAMPING = 0.6
DIAGONAL = SHIFT - 1.5 * CENTER_TAP
CELLS = 384 * 64 * 256
NORB = 4
NTYPES = 8

SIDE = tuple(-0.5 * w for w in SIDE_TAPS)
CENTER = -1.5 * CENTER_TAP
W = DAMPING / DIAGONAL
P1, P2, P3 = 3.0 * W, -3.0 * W * W, W * W * W

PL, RW, CO = 12, 16, 128
H = 6
PAIRS = [(i, j) for i in range(NORB) for j in range(i + 1)]


def iota(shape, dim):
    return lax.broadcasted_iota(jnp.int32, shape, dim)


def taps_at(distance, centre):
    out = jnp.zeros(distance.shape, jnp.float32)
    if centre is not None:
        out = jnp.where(distance == 0, jnp.float32(centre), out)
    for n, w in enumerate(SIDE, 1):
        out = jnp.where(distance == n, jnp.float32(w), out)
    return out


def dot(a, b, ca, cb):
    return lax.dot_general(
        a, b, (((ca,), (cb,)), ((), ())), precision=HIGH, preferred_element_type=jnp.float32
    )


def cholesky(s):
    low = {}
    inv = []
    for i in range(NORB):
        for j in range(i):
            t = s[i, j]
            for k in range(j):
                t = t - low[i, k] * low[j, k]
            low[i, j] = t * inv[j]
        t = s[i, i]
        for k in range(i):
            t = t - low[i, k] * low[i, k]
        root = jnp.sqrt(t)
        low[i, i] = root
        inv.append(1.0 / root)
    return low, inv


def kernel(
    x_hbm, type_hbm, table_hbm, step_hbm, out_ref,
    x_ref, type_ref, table_ref, step_ref, own_ref, pick_ref, spread_ref,
    xf, wf, nf, mf, vs, vf, base, vv, new, zz, zd_out, zd, zs, zr, gram, coef, ra, rb,
    in_sem, t_send, t_recv, d_send, d_recv, v_send, v_recv, h_send, h_recv, b_send, b_recv, r_send, r_recv,
):
    s = lax.axis_index("space")
    o = lax.axis_index("orb")
    h, c, q, x = o // 2, o % 2, s // 4, s % 4
    side = (c + q) % 2
    host = (x // 2 + q) % 2
    mine = c == host
    link = 2 * q + side
    has_left, has_right = link > 0, link < 31

    def device(hh, cc, qq, xx):
        return (2 * hh + cc, 4 * qq + xx)

    def along(n):
        n = n % 32
        return device(h, (n + n // 2) % 2, n // 2, x)

    left, right = along(link + 31), along(link + 1)
    up = device(h, c, q, (x + 3) % 4)
    down = device(h, c, q, (x + 1) % 4)
    across = device(1 - h, c, q, x)

    me1 = (x * 2 + h) * 2 + c
    me2 = q

    def peer1(k):
        i = (me1 + k) % 16
        return device((i // 2) % 2, i % 2, q, i // 4)

    def peer2(k):
        return device(h, c, (me2 + k) % 16, x)

    loads = [
        pltpu.make_async_copy(src, dst, in_sem.at[n])
        for n, (src, dst) in enumerate(
            ((x_hbm, x_ref), (type_hbm, type_ref), (table_hbm, table_ref), (step_hbm, step_ref))
        )
    ]
    for cp in loads:
        cp.start()

    barrier = pltpu.get_barrier_semaphore()

    def hello(k, carry):
        pl.semaphore_signal(barrier, inc=1, device_id=peer1(k), device_id_type=MESH)
        pl.semaphore_signal(barrier, inc=1, device_id=peer2(k), device_id_type=MESH)
        return carry

    lax.fori_loop(1, 16, hello, 0)

    own_ref[...] = taps_at(jnp.abs(iota((CO, CO), 0) - iota((CO, CO), 1)), CENTER)
    row, col = iota((16, CO), 0), iota((16, CO), 1)
    target = jnp.where(row < H, CO - H + row, jnp.where(row < 2 * H, row - H, -1))
    pick_ref[...] = jnp.where(col == target, jnp.float32(1.0), jnp.float32(0.0))
    spread_ref[...] = taps_at(
        jnp.where(row < H, col + H - row, jnp.where(row < 2 * H, CO + row - H - col, 0)), None
    )
    gram[...] = jnp.zeros(gram.shape, jnp.float32)
    for f in (xf, wf, nf, mf):
        @pl.when(jnp.logical_not(has_left))
        def _():
            f[:, 0:H] = jnp.zeros((NORB, H, RW + 16, CO), jnp.float32)

        @pl.when(jnp.logical_not(has_right))
        def _():
            f[:, H + PL:] = jnp.zeros((NORB, H, RW + 16, CO), jnp.float32)

    def rows_of(xx):
        return pl.ds(pl.multiple_of(16 * xx, 16), 16)

    def cols_of(hh):
        return pl.ds(pl.multiple_of(CO * hh, CO), CO)

    def part(ref, xx, hh):
        return ref.at[:, rows_of(xx), cols_of(hh)]

    def remote(src, dst, ss, rs, dev):
        return pltpu.make_async_remote_copy(
            src_ref=src, dst_ref=dst, send_sem=ss, recv_sem=rs, device_id=dev, device_id_type=MESH
        )

    def guarded(cond, fn):
        if cond is None:
            fn()
        else:
            pl.when(cond)(fn)

    loads[0].wait()
    for k in range(4):
        edge = x_ref[:, rows_of((x + k) % 4), cols_of(1 - h)].reshape(6 * RW, CO)
        zd_out[k, :, 0:6 * RW] = dot(pick_ref[...], edge, 1, 1)

    for cp in loads[1:]:
        cp.wait()
    kinds = type_ref[...]
    potential = jnp.zeros(kinds.shape, jnp.float32)
    for kind in range(NTYPES):
        potential = jnp.where(kinds == kind, table_ref[kind], potential)
    vs[...] = potential

    pl.semaphore_wait(barrier, 30)

    half = x % 2

    def scatter(j, k):
        hh, xx = (h + j) % 2, (x + k) % 4
        n = 4 * j + k
        return part(x_ref, xx, hh), xf.at[o, pl.ds(H + 6 * half, 6), pl.ds(8, 16)], t_send.at[n], t_recv.at[2 * o + half], device(hh, host, q, xx)

    def edges(k):
        return zd_out.at[k], zd.at[c, half], d_send.at[k], d_recv.at[2 * c + half], device(h, host, q, (x + k) % 4)

    def potentials(k, n):
        xx = (x + k) % 4
        return part(vs, xx, h), vf.at[pl.ds(6 * half, 6)], v_send.at[n], v_recv.at[half], device(h, host, q, xx)

    def local_or_remote(a):
        @pl.when(mine)
        def _():
            pltpu.make_async_copy(a[0], a[1], a[3]).start()

        @pl.when(jnp.logical_not(mine))
        def _():
            remote(*a).start()

    for k in (2, 1, 3, 0):
        remote(*scatter(1, k)).start()
    for k in (2, 1, 3, 0):
        if k == 0:
            local_or_remote(scatter(0, 0))
            local_or_remote(edges(0))
        else:
            remote(*scatter(0, k)).start()
            remote(*edges(k)).start()

    @pl.when(mine)
    def _():
        a = potentials(0, 0)
        pltpu.make_async_copy(a[0], a[1], a[3]).start()
        remote(*potentials(2, 1)).start()

    @pl.when(jnp.logical_not(mine))
    def _():
        remote(*potentials(1, 0)).start()
        remote(*potentials(3, 1)).start()

    A, B = h, 1 - h

    def halo_copies(f, r, pair):
        at = pl.ds(2 * pair, 2)
        m = 10 * r + 5 * pair
        return (
            (has_left, remote(f.at[at, H:2 * H, 8:8 + RW], f.at[at, H + PL:, 8:8 + RW], h_send.at[m], h_recv.at[m + 1], left)),
            (has_right, remote(f.at[at, PL:PL + H, 8:8 + RW], f.at[at, 0:H, 8:8 + RW], h_send.at[m + 1], h_recv.at[m], right)),
            (None, remote(f.at[at, H:H + PL, 8:14], f.at[at, H:H + PL, 24:30], h_send.at[m + 2], h_recv.at[m + 3], up)),
            (None, remote(f.at[at, H:H + PL, 18:24], f.at[at, H:H + PL, 2:8], h_send.at[m + 3], h_recv.at[m + 2], down)),
            (None, remote(zs.at[r, pair], zr.at[r, pair], h_send.at[m + 4], h_recv.at[m + 4], across)),
        )

    def share(f, pair):
        return f[pl.ds(2 * pair, 2), H:H + PL, 8:8 + RW].reshape(2 * PL * RW, CO)

    def halo_start(f, r, pair, with_z=True):
        copies = halo_copies(f, r, pair)
        flat = share(f, pair)
        if with_z:
            zs[r, pair] = dot(pick_ref[...], flat, 1, 1)
            copies[4][1].start()
        for n in (0, 1, 2, 3):
            guarded(copies[n][0], copies[n][1].start)
        zz[r, pair] = dot(flat, own_ref[...], 1, 0)

    def halo_finish(f, r, pair, with_z=True):
        copies = halo_copies(f, r, pair)
        guarded(has_left, copies[1][1].wait_recv)
        guarded(has_right, copies[0][1].wait_recv)
        copies[2][1].wait_recv()
        copies[3][1].wait_recv()
        if with_z:
            copies[4][1].wait_recv()
            zz[r, pair] += dot(zr[r, pair], spread_ref[...], 0, 0)

    def halo_sent(f, r, pair, with_z=True):
        for cond, cp in halo_copies(f, r, pair)[:5 if with_z else 4]:
            guarded(cond, cp.wait_send)

    def kinetic(f, r, pair, i, p):
        total = zz[r, pair, pl.ds(pl.multiple_of((i * PL + p) * RW, RW), RW)]
        i = 2 * pair + i
        for n in range(1, H + 1):
            near = f[i, p + H + n, 8:8 + RW] + f[i, p + H - n, 8:8 + RW]
            near = near + f[i, p + H, 8 + n:8 + RW + n] + f[i, p + H, 8 - n:8 + RW - n]
            total = total + SIDE[n - 1] * near
        return total

    def each(fn, pair):
        def step(n, carry):
            fn(pair, n // PL, n % PL)
            return carry
        lax.fori_loop(0, 2 * PL, step, 0, unroll=4)

    def each_plane(fn, init=0):
        return lax.fori_loop(0, PL, fn, init, unroll=2)

    def reduce_start(v, buf, send, recv, me, peer):
        buf[me] = v

        def go(k, carry):
            remote(buf.at[me], buf.at[me], send, recv, peer(k)).start()
            return carry

        lax.fori_loop(1, 16, go, 0)

    def reduce_finish(buf, send, recv, peer):
        cp = remote(buf.at[pl.ds(0, 15)], buf.at[pl.ds(0, 15)], send, recv, peer(1))
        cp.wait_send()
        cp.wait_recv()
        return jnp.sum(buf[...], axis=0)

    def local_sums(rows):
        for n, v in enumerate(rows):
            gram[n:n + 1] = jnp.sum(v, axis=0, keepdims=True)
        return dot(jnp.ones((8, CO), jnp.float32), gram[...], 1, 1)[0:1]

    def spread_out(v, n):
        return jnp.broadcast_to(v[:, n:n + 1], (8, CO)) * (1.0 / CELLS)

    def wide(f, i, p):
        return f[i, p + H, 8:8 + RW].reshape(2, 8, CO)

    def narrow(f, i, p):
        return f[i, p].reshape(2, 8, CO)

    def first(pair, i, p):
        k = kinetic(xf, 0, pair, i, p)
        i = 2 * pair + i
        v = xf[i, p + H, 8:8 + RW]
        wf[i, p + H, 8:8 + RW] = k + vf[p] * v
        nf[i, p + H, 8:8 + RW] = k + SHIFT * v

    def second(pair, i, p):
        k = kinetic(wf, 1, pair, i, p)
        i = 2 * pair + i
        mf[i, p + H, 8:8 + RW] = k + SHIFT * wf[i, p + H, 8:8 + RW]

    def smooth_x(pair, i, p):
        k = kinetic(nf, 2, pair, i, p)
        i = 2 * pair + i
        vv[i, p] = P1 * xf[i, p + H, 8:8 + RW] + (P2 + SHIFT * P3) * nf[i, p + H, 8:8 + RW] + P3 * k

    def smooth_w(pair, i, p):
        k = kinetic(mf, 3, pair, i, p)
        i = 2 * pair + i
        t = P1 * wf[i, p + H, 8:8 + RW] + (P2 + SHIFT * P3) * mf[i, p + H, 8:8 + RW] + P3 * k
        base[i, p] = xf[i, p + H, 8:8 + RW] - step_ref[i] * t

    def arrived(pair):
        for i in range(2):
            for p in range(2):
                ref = xf.at[2 * pair + i, pl.ds(H + 6 * p, 6), pl.ds(8, 16)]
                remote(ref, ref, t_send.at[0], t_recv.at[2 * (2 * pair + i) + p], across).wait_recv()

    arrived(A)
    halo_start(xf, 0, A)
    arrived(B)
    halo_start(xf, 0, B, False)
    for i in range(2):
        for p in range(2):
            remote(zd.at[i, p], zd.at[i, p], d_send.at[0], d_recv.at[2 * i + p], across).wait_recv()
            at = pl.ds((2 * i + p) * 6 * RW, 6 * RW)
            zz[0, A, at] += dot(zd[i, p][:, 0:6 * RW], spread_ref[...], 0, 0)
    for p in range(2):
        remote(vf.at[pl.ds(6 * p, 6)], vf.at[pl.ds(6 * p, 6)], v_send.at[0], v_recv.at[p], across).wait_recv()
    halo_finish(xf, 0, A, False)
    each(first, A)
    halo_start(wf, 1, A)
    halo_finish(xf, 0, B)
    each(first, B)
    halo_start(wf, 1, B)
    halo_start(nf, 2, A)
    halo_start(nf, 2, B)

    def products(p, acc):
        xs = [wide(xf, i, p) for i in range(NORB)]
        ws = [wide(wf, i, p) for i in range(NORB)]
        acc = list(acc)
        for n, (i, j) in enumerate(PAIRS):
            acc[n] = acc[n] + jnp.sum(xs[i] * xs[j], axis=0)
        for j in range(NORB):
            for i in range(NORB):
                n = 10 + 4 * j + i
                acc[n] = acc[n] + jnp.sum(xs[j] * ws[i], axis=0)
        return tuple(acc)

    zero = jnp.zeros((8, CO), jnp.float32)
    acc = each_plane(products, (zero,) * 26)
    reduce_start(local_sums(acc), ra.at[0], r_send.at[0], r_recv.at[0], me1, peer1)

    halo_finish(wf, 1, A)
    each(second, A)
    halo_start(mf, 3, A)
    halo_finish(wf, 1, B)
    each(second, B)
    halo_start(mf, 3, B)
    halo_finish(nf, 2, A)
    each(smooth_x, A)
    v = reduce_finish(ra.at[0], r_send.at[0], r_recv.at[0], peer1)
    reduce_start(v, rb.at[0], r_send.at[1], r_recv.at[1], me2, peer2)
    halo_finish(nf, 2, B)
    each(smooth_x, B)
    halo_finish(mf, 3, A)
    each(smooth_w, A)
    halo_finish(mf, 3, B)
    each(smooth_w, B)

    v = reduce_finish(rb.at[0], r_send.at[1], r_recv.at[1], peer2)
    margin = {(i, j): spread_out(v, n) for n, (i, j) in enumerate(PAIRS)}
    low, inv = cholesky(margin)
    for i in range(NORB):
        y = []
        for j in range(NORB):
            t = spread_out(v, 10 + 4 * j + i)
            for k in range(j):
                t = t - low[j, k] * y[k]
            y.append(t * inv[j])
        for j in reversed(range(NORB)):
            t = y[j]
            for k in range(j + 1, NORB):
                t = t - low[k, j] * y[k]
            y[j] = t * inv[j]
            coef[4 * i + j] = step_ref[i] * y[j]

    def move(p, acc):
        vs4 = [narrow(vv, j, p) for j in range(NORB)]
        ms = []
        for i in range(NORB):
            t = narrow(base, i, p)
            for j in range(NORB):
                t = t + coef[4 * i + j] * vs4[j]
            base[i, p] = t.reshape(RW, CO)
            ms.append(t)
        return tuple(a + jnp.sum(ms[i] * ms[j], axis=0) for a, (i, j) in zip(acc, PAIRS))

    acc = each_plane(move, (zero,) * 10)
    reduce_start(local_sums(acc), ra.at[1], r_send.at[2], r_recv.at[2], me1, peer1)
    v = reduce_finish(ra.at[1], r_send.at[2], r_recv.at[2], peer1)
    reduce_start(v, rb.at[1], r_send.at[3], r_recv.at[3], me2, peer2)
    v = reduce_finish(rb.at[1], r_send.at[3], r_recv.at[3], peer2)
    low, inv = cholesky({(i, j): spread_out(v, n) for n, (i, j) in enumerate(PAIRS)})
    lowinv = {}
    for j in range(NORB):
        lowinv[j, j] = inv[j]
        for i in range(j + 1, NORB):
            t = low[i, j] * lowinv[j, j]
            for k in range(j + 1, i):
                t = t + low[i, k] * lowinv[k, j]
            lowinv[i, j] = -t * inv[i]
    for n, ij in enumerate(PAIRS):
        coef[n] = lowinv[ij]

    def rotate(p, carry):
        ms = [narrow(base, j, p) for j in range(NORB)]
        for i in range(NORB):
            t = None
            for n, (a, j) in enumerate(PAIRS):
                if a == i:
                    term = coef[n] * ms[j]
                    t = term if t is None else t + term
            new[i, p] = t.reshape(RW, CO)
        return carry

    each_plane(rotate)

    def back(j, i, m):
        hh, cc, pp = (h + j) % 2, (c + i) % 2, (x + m) % 2
        return new.at[2 * hh + cc, pl.ds(6 * pp, 6)], part(out_ref, x, h), b_send.at[4 * j + 2 * i + m], b_recv.at[2 * x + h], device(hh, cc, q, 2 * side + pp)

    order = [(j, i, m) for j in (1, 0) for i in (1, 0) for m in (1, 0)]
    for jim in order:
        a = back(*jim)
        if jim == (0, 0, 0):
            local_or_remote(a)
        else:
            remote(*a).start()

    unless_mine = jnp.logical_not(mine)
    for k in range(4):
        remote(*scatter(1, k)).wait_send()
        guarded(unless_mine if k == 0 else None, remote(*scatter(0, k)).wait_send)
        guarded(unless_mine if k == 0 else None, remote(*edges(k)).wait_send)

    @pl.when(mine)
    def _():
        remote(*potentials(2, 1)).wait_send()

    @pl.when(unless_mine)
    def _():
        remote(*potentials(1, 0)).wait_send()
        remote(*potentials(3, 1)).wait_send()

    for r, f in enumerate((xf, wf, nf, mf)):
        halo_sent(f, r, A)
        halo_sent(f, r, B, r > 0)
    for jim in order:
        guarded(unless_mine if jim == (0, 0, 0) else None, remote(*back(*jim)).wait_send)
    for xx in range(4):
        for hh in range(2):
            dst = out_ref.at[:, pl.ds(16 * xx, 16), pl.ds(CO * hh, CO)]
            remote(dst, dst, b_send.at[0], b_recv.at[2 * xx + hh], across).wait_recv()


def body(orbitals, atom_type, type_table, step_length):
    shape = orbitals.shape
    slab = shape[1:]
    anywhere = pl.BlockSpec(memory_space=pl.ANY)
    f32 = jnp.float32
    share = (NORB, PL, RW, CO)
    wide = (NORB, PL + 2 * H, RW + 16, CO)
    rows = 2 * PL * RW
    dma = pltpu.SemaphoreType.DMA

    def vmem(*shape):
        return pltpu.VMEM(shape, f32)

    out = pl.pallas_call(
        kernel,
        out_shape=jax.ShapeDtypeStruct(slab, f32),
        in_specs=[anywhere] * 4,
        out_specs=pl.BlockSpec(memory_space=pltpu.VMEM),
        scratch_shapes=[
            vmem(*slab), pltpu.VMEM(slab, jnp.int32), pltpu.SMEM((NTYPES,), f32), pltpu.SMEM((NORB,), f32),
            vmem(CO, CO), vmem(16, CO), vmem(16, CO),
            vmem(*wide), vmem(*wide), vmem(*wide), vmem(*wide),
            vmem(*slab), vmem(PL, RW, CO), vmem(*share), vmem(*share), vmem(*share),
            vmem(4, 2, rows, CO), vmem(4, 16, CO), vmem(2, 2, 16, CO),
            vmem(4, 2, 16, rows), vmem(4, 2, 16, rows),
            vmem(CO, CO), vmem(16, 8, CO), vmem(2, 16, 1, CO), vmem(2, 16, 1, CO),
            dma((4,)), dma((8,)), dma((8,)), dma((4,)), dma((4,)), dma((2,)), dma((2,)),
            dma((40,)), dma((40,)), dma((8,)), dma((8,)), dma((4,)), dma((4,)),
        ],
        compiler_params=pltpu.CompilerParams(
            collective_id=0, has_side_effects=True, vmem_limit_bytes=55993958
        ),
        name="step",
    )(orbitals.reshape(slab), atom_type, type_table, step_length)
    return out.reshape(shape)


def solution(mesh):
    in_specs = (P("orb", "space", None, None), P("space", None, None), P(), P())
    out_specs = P("orb", "space", None, None)
    return jax.shard_map(body, mesh=mesh, in_specs=in_specs, out_specs=out_specs, check_vma=False)
```

time: 84 us -> 71.1 us (0.85)
  Pallas kernels: 78.1 us -> 69.5 us
  local copies, waits for them, and re-layouts: 5.64 us -> 1.42 us
    pallas_call x1, Pallas kernels: 78.1 us -> 69.5 us  [body(): pl.pallas_call(kernel, out_shape=jax.ShapeDtypeStruct(slab, f32), in_spec...]
    unnamed x15 -> x5, local copies, waits for them, and re-layouts: 5.64 us -> 1.42 us
where the time goes in v2:
time: 71.1 us; the launch traced here: 71 us
  Pallas kernels  69.5 us (98%)
  local copies, waits for them, and re-layouts  1.42 us (2%)
    pallas_call x1, Pallas kernels, body(): pl.pallas_call(kernel, out_shape=jax.ShapeDtypeStruct(slab, f32), in_spec...  69.5 us

profile of v2, /device:TPU:64, one launch (start us, length us, event | category | flops | bytes accessed | tf_op | source)
XLA Modules:
  0.0 71.0 jit_solution(8820209187393526132)
XLA Ops:
  0.0 0.0 copy-start.1
  0.0 0.0 copy-start
  0.0 0.7 copy-done.1
  0.7 0.0 copy-done
  0.7 69.5 %step.1 = f32[6,64,256]{2,1,0:T(8,128)S(1)} custom-call(f32[6,64,256]{2,1,0:T(8,128)} %bitcast.3, s32[6,64,256]{2,1,0:T(8,128)} %type_hbm.1, f32[8]{0:T(128)S(1)} %copy-done, f32[4]{0:T(128)S(1)} %copy-done.1), custom_call_target="tpu_custom_call" | custom-call | tf_op jit(solution)/shard_map/step/pallas_call | solution.py:495
  70.2 0.7 %copy.6 = f32[1,6,64,256]{3,2,1,0:T(8,128)} copy(f32[1,6,64,256]{3,2,1,0:T(8,128)S(1)} %bitcast.2) | data formatting | bytes 786432
Async XLA Ops:
  0.0 0.7 copy-start.1
  0.0 0.7 copy-start

commit v3 on v2

--- a/solution.py
+++ b/solution.py
@@ -1,3 +1,5 @@
+import functools
+
 import jax
 import jax.numpy as jnp
 from jax import lax
@@ -23,6 +25,8 @@
 
 PL, RW, CO = 12, 16, 128
 H = 6
+GRAM = 32
+FAR_FIRST = (10, 6, 2, 14, 11, 7, 3, 15, 8, 9, 4, 12, 5, 13, 1)
 PAIRS = [(i, j) for i in range(NORB) for j in range(i + 1)]
 
 
@@ -43,6 +47,31 @@
     return lax.dot_general(
         a, b, (((ca,), (cb,)), ((), ())), precision=HIGH, preferred_element_type=jnp.float32
     )
+
+
+def pieces(a):
+    high = a.astype(jnp.bfloat16)
+    return high, (a - high.astype(jnp.float32)).astype(jnp.bfloat16)
+
+
+def joined(a, axis):
+    return jnp.concatenate(pieces(a), axis=axis)
+
+
+def dot16(a, b, ca, cb):
+    return lax.dot_general(a, b, (((ca,), (cb,)), ((), ())), preferred_element_type=jnp.float32)
+
+
+def table(a):
+    high, low = pieces(a)
+    none = jnp.zeros(a.shape, jnp.bfloat16)
+    return jnp.concatenate(
+        [jnp.concatenate([high, high], axis=0), jnp.concatenate([low, none], axis=0)], axis=1
+    )
+
+
+def both(a):
+    return a[:, :CO] + a[:, CO:]
 
 
 def cholesky(s):
@@ -111,29 +140,9 @@
 
     barrier = pltpu.get_barrier_semaphore()
 
-    def hello(k, carry):
-        pl.semaphore_signal(barrier, inc=1, device_id=peer1(k), device_id_type=MESH)
-        pl.semaphore_signal(barrier, inc=1, device_id=peer2(k), device_id_type=MESH)
-        return carry
-
-    lax.fori_loop(1, 16, hello, 0)
-
-    own_ref[...] = taps_at(jnp.abs(iota((CO, CO), 0) - iota((CO, CO), 1)), CENTER)
-    row, col = iota((16, CO), 0), iota((16, CO), 1)
-    target = jnp.where(row < H, CO - H + row, jnp.where(row < 2 * H, row - H, -1))
-    pick_ref[...] = jnp.where(col == target, jnp.float32(1.0), jnp.float32(0.0))
-    spread_ref[...] = taps_at(
-        jnp.where(row < H, col + H - row, jnp.where(row < 2 * H, CO + row - H - col, 0)), None
-    )
-    gram[...] = jnp.zeros(gram.shape, jnp.float32)
-    for f in (xf, wf, nf, mf):
-        @pl.when(jnp.logical_not(has_left))
-        def _():
-            f[:, 0:H] = jnp.zeros((NORB, H, RW + 16, CO), jnp.float32)
-
-        @pl.when(jnp.logical_not(has_right))
-        def _():
-            f[:, H + PL:] = jnp.zeros((NORB, H, RW + 16, CO), jnp.float32)
+    for peer in (peer1, peer2):
+        for k in FAR_FIRST:
+            pl.semaphore_signal(barrier, inc=1, device_id=peer(k), device_id_type=MESH)
 
     def rows_of(xx):
         return pl.ds(pl.multiple_of(16 * xx, 16), 16)
@@ -155,10 +164,64 @@
         else:
             pl.when(cond)(fn)
 
+    half = x % 2
+
+    def scatter(j, k):
+        hh, xx = (h + j) % 2, (x + k) % 4
+        n = 4 * j + k
+        return part(x_hbm, xx, hh), xf.at[o, pl.ds(H + 6 * half, 6), pl.ds(8, 16)], t_send.at[n], t_recv.at[2 * o + half], device(hh, host, q, xx)
+
+    def edges(k):
+        return zd_out.at[k], zd.at[c, half], d_send.at[k], d_recv.at[2 * c + half], device(h, host, q, (x + k) % 4)
+
+    def potentials(k, n):
+        xx = (x + k) % 4
+        return part(vs, xx, h), vf.at[pl.ds(6 * half, 6)], v_send.at[n], v_recv.at[half], device(h, host, q, xx)
+
+    def local_or_remote(a):
+        @pl.when(mine)
+        def _():
+            pltpu.make_async_copy(a[0], a[1], a[3]).start()
+
+        @pl.when(jnp.logical_not(mine))
+        def _():
+            remote(*a).start()
+
+    pl.semaphore_wait(barrier, 30)
+
+    for k in (2, 1, 3, 0):
+        remote(*scatter(1, k)).start()
+    for k in (2, 1, 3):
+        remote(*scatter(0, k)).start()
+    local_or_remote(scatter(0, 0))
+
+    own_ref[...] = table(taps_at(jnp.abs(iota((CO, CO), 0) - iota((CO, CO), 1)), CENTER))
+    row, col = iota((16, CO), 0), iota((16, CO), 1)
+    target = jnp.where(row < H, CO - H + row, jnp.where(row < 2 * H, row - H, -1))
+    pick = jnp.where(col == target, jnp.float32(1.0), jnp.float32(0.0)).astype(jnp.bfloat16)
+    pick_ref[...] = jnp.concatenate([pick, pick], axis=1)
+    spread_ref[...] = table(taps_at(
+        jnp.where(row < H, col + H - row, jnp.where(row < 2 * H, CO + row - H - col, 0)), None
+    ))
+    gram[...] = jnp.zeros(gram.shape, jnp.float32)
+    zr[:, :, :, 2 * H:] = jnp.zeros((4, 2, 3, 16 - 2 * H, CO), jnp.float32)
+    for f in (xf, wf, nf, mf):
+        @pl.when(jnp.logical_not(has_left))
+        def _():
+            f[:, 0:H] = jnp.zeros((NORB, H, RW + 16, CO), jnp.float32)
+
+        @pl.when(jnp.logical_not(has_right))
+        def _():
+            f[:, H + PL:] = jnp.zeros((NORB, H, RW + 16, CO), jnp.float32)
+
     loads[0].wait()
     for k in range(4):
         edge = x_ref[:, rows_of((x + k) % 4), cols_of(1 - h)].reshape(6 * RW, CO)
-        zd_out[k, :, 0:6 * RW] = dot(pick_ref[...], edge, 1, 1)
+        zd_out[k, :, 0:6 * RW] = dot16(pick_ref[...], joined(edge, 1), 1, 1)
+
+    for k in (2, 1, 3):
+        remote(*edges(k)).start()
+    local_or_remote(edges(0))
 
     for cp in loads[1:]:
         cp.wait()
@@ -167,41 +230,6 @@
     for kind in range(NTYPES):
         potential = jnp.where(kinds == kind, table_ref[kind], potential)
     vs[...] = potential
-
-    pl.semaphore_wait(barrier, 30)
-
-    half = x % 2
-
-    def scatter(j, k):
-        hh, xx = (h + j) % 2, (x + k) % 4
-        n = 4 * j + k
-        return part(x_ref, xx, hh), xf.at[o, pl.ds(H + 6 * half, 6), pl.ds(8, 16)], t_send.at[n], t_recv.at[2 * o + half], device(hh, host, q, xx)
-
-    def edges(k):
-        return zd_out.at[k], zd.at[c, half], d_send.at[k], d_recv.at[2 * c + half], device(h, host, q, (x + k) % 4)
-
-    def potentials(k, n):
-        xx = (x + k) % 4
-        return part(vs, xx, h), vf.at[pl.ds(6 * half, 6)], v_send.at[n], v_recv.at[half], device(h, host, q, xx)
-
-    def local_or_remote(a):
-        @pl.when(mine)
-        def _():
-            pltpu.make_async_copy(a[0], a[1], a[3]).start()
-
-        @pl.when(jnp.logical_not(mine))
-        def _():
-            remote(*a).start()
-
-    for k in (2, 1, 3, 0):
-        remote(*scatter(1, k)).start()
-    for k in (2, 1, 3, 0):
-        if k == 0:
-            local_or_remote(scatter(0, 0))
-            local_or_remote(edges(0))
-        else:
-            remote(*scatter(0, k)).start()
-            remote(*edges(k)).start()
 
     @pl.when(mine)
     def _():
@@ -224,7 +252,7 @@
             (has_right, remote(f.at[at, PL:PL + H, 8:8 + RW], f.at[at, 0:H, 8:8 + RW], h_send.at[m + 1], h_recv.at[m], right)),
             (None, remote(f.at[at, H:H + PL, 8:14], f.at[at, H:H + PL, 24:30], h_send.at[m + 2], h_recv.at[m + 3], up)),
             (None, remote(f.at[at, H:H + PL, 18:24], f.at[at, H:H + PL, 2:8], h_send.at[m + 3], h_recv.at[m + 2], down)),
-            (None, remote(zs.at[r, pair], zr.at[r, pair], h_send.at[m + 4], h_recv.at[m + 4], across)),
+            (None, remote(zs.at[r, pair, :, 0:2 * H], zr.at[r, pair, :, 0:2 * H], h_send.at[m + 4], h_recv.at[m + 4], across)),
         )
 
     def share(f, pair):
@@ -232,13 +260,15 @@
 
     def halo_start(f, r, pair, with_z=True):
         copies = halo_copies(f, r, pair)
-        flat = share(f, pair)
+        flat = joined(share(f, pair), 1)
         if with_z:
-            zs[r, pair] = dot(pick_ref[...], flat, 1, 1)
+            edge = dot16(pick_ref[...], flat, 1, 1)
+            for b in range(3):
+                zs[r, pair, b] = edge[:, CO * b:CO * b + CO]
             copies[4][1].start()
         for n in (0, 1, 2, 3):
             guarded(copies[n][0], copies[n][1].start)
-        zz[r, pair] = dot(flat, own_ref[...], 1, 0)
+        zz[r, pair] = both(dot16(flat, own_ref[...], 1, 0))
 
     def halo_finish(f, r, pair, with_z=True):
         copies = halo_copies(f, r, pair)
@@ -246,15 +276,25 @@
         guarded(has_right, copies[0][1].wait_recv)
         copies[2][1].wait_recv()
         copies[3][1].wait_recv()
+        if with_z == "late":
+            def step(n, carry):
+                at = pl.ds(pl.multiple_of(n * RW, RW), RW)
+                zz[r, pair, at] = taps_xy(f, r, pair, n // PL, n % PL)
+                return carry
+
+            lax.fori_loop(0, 2 * PL, step, 0, unroll=4)
         if with_z:
             copies[4][1].wait_recv()
-            zz[r, pair] += dot(zr[r, pair], spread_ref[...], 0, 0)
+            zz[r, pair] += both(dot16(joined(jnp.concatenate([zr[r, pair, b] for b in range(3)], axis=1), 0), spread_ref[...], 0, 0))
 
     def halo_sent(f, r, pair, with_z=True):
         for cond, cp in halo_copies(f, r, pair)[:5 if with_z else 4]:
             guarded(cond, cp.wait_send)
 
-    def kinetic(f, r, pair, i, p):
+    def kinetic(r, pair, i, p):
+        return zz[r, pair, pl.ds(pl.multiple_of((i * PL + p) * RW, RW), RW)]
+
+    def taps_xy(f, r, pair, i, p):
         total = zz[r, pair, pl.ds(pl.multiple_of((i * PL + p) * RW, RW), RW)]
         i = 2 * pair + i
         for n in range(1, H + 1):
@@ -275,11 +315,8 @@
     def reduce_start(v, buf, send, recv, me, peer):
         buf[me] = v
 
-        def go(k, carry):
+        for k in FAR_FIRST:
             remote(buf.at[me], buf.at[me], send, recv, peer(k)).start()
-            return carry
-
-        lax.fori_loop(1, 16, go, 0)
 
     def reduce_finish(buf, send, recv, peer):
         cp = remote(buf.at[pl.ds(0, 15)], buf.at[pl.ds(0, 15)], send, recv, peer(1))
@@ -287,10 +324,14 @@
         cp.wait_recv()
         return jnp.sum(buf[...], axis=0)
 
+    def local_total():
+        v = dot(jnp.ones((8, CO), jnp.float32), gram[...], 1, 1)[0:1]
+        return jnp.concatenate([v, jnp.zeros((1, CO - GRAM), jnp.float32)], axis=1)
+
     def local_sums(rows):
         for n, v in enumerate(rows):
             gram[n:n + 1] = jnp.sum(v, axis=0, keepdims=True)
-        return dot(jnp.ones((8, CO), jnp.float32), gram[...], 1, 1)[0:1]
+        return local_total()
 
     def spread_out(v, n):
         return jnp.broadcast_to(v[:, n:n + 1], (8, CO)) * (1.0 / CELLS)
@@ -302,24 +343,24 @@
         return f[i, p].reshape(2, 8, CO)
 
     def first(pair, i, p):
-        k = kinetic(xf, 0, pair, i, p)
+        k = taps_xy(xf, 0, pair, i, p)
         i = 2 * pair + i
         v = xf[i, p + H, 8:8 + RW]
         wf[i, p + H, 8:8 + RW] = k + vf[p] * v
         nf[i, p + H, 8:8 + RW] = k + SHIFT * v
 
     def second(pair, i, p):
-        k = kinetic(wf, 1, pair, i, p)
+        k = taps_xy(wf, 1, pair, i, p)
         i = 2 * pair + i
         mf[i, p + H, 8:8 + RW] = k + SHIFT * wf[i, p + H, 8:8 + RW]
 
     def smooth_x(pair, i, p):
-        k = kinetic(nf, 2, pair, i, p)
+        k = taps_xy(nf, 2, pair, i, p)
         i = 2 * pair + i
         vv[i, p] = P1 * xf[i, p + H, 8:8 + RW] + (P2 + SHIFT * P3) * nf[i, p + H, 8:8 + RW] + P3 * k
 
     def smooth_w(pair, i, p):
-        k = kinetic(mf, 3, pair, i, p)
+        k = taps_xy(mf, 3, pair, i, p)
         i = 2 * pair + i
         t = P1 * wf[i, p + H, 8:8 + RW] + (P2 + SHIFT * P3) * mf[i, p + H, 8:8 + RW] + P3 * k
         base[i, p] = xf[i, p + H, 8:8 + RW] - step_ref[i] * t
@@ -338,33 +379,40 @@
         for p in range(2):
             remote(zd.at[i, p], zd.at[i, p], d_send.at[0], d_recv.at[2 * i + p], across).wait_recv()
             at = pl.ds((2 * i + p) * 6 * RW, 6 * RW)
-            zz[0, A, at] += dot(zd[i, p][:, 0:6 * RW], spread_ref[...], 0, 0)
+            zz[0, A, at] += both(dot16(joined(zd[i, p][:, 0:6 * RW], 0), spread_ref[...], 0, 0))
     for p in range(2):
         remote(vf.at[pl.ds(6 * p, 6)], vf.at[pl.ds(6 * p, 6)], v_send.at[0], v_recv.at[p], across).wait_recv()
     halo_finish(xf, 0, A, False)
     each(first, A)
     halo_start(wf, 1, A)
+    halo_start(nf, 2, A)
+
+    def products(pair, with_margin, p, acc):
+        xs = [wide(xf, i, p) for i in range(NORB)]
+        ws = [wide(wf, 2 * pair + i, p) for i in range(2)]
+        terms = [xs[i] * xs[j] for i, j in PAIRS] if with_margin else []
+        terms += [xs[j] * w for j in range(NORB) for w in ws]
+        return tuple(a + jnp.sum(v, axis=0) for a, v in zip(acc, terms))
+
+    zero = jnp.zeros((8, CO), jnp.float32)
+    early = each_plane(functools.partial(products, A, True), (zero,) * 18)
+    for n in range(10):
+        gram[n:n + 1] = jnp.sum(early[n], axis=0, keepdims=True)
+    sums = {}
     halo_finish(xf, 0, B)
     each(first, B)
     halo_start(wf, 1, B)
-    halo_start(nf, 2, A)
+    acc = each_plane(functools.partial(products, B, False), (zero,) * 8)
+    late = acc
+    for j in range(NORB):
+        for i in range(2):
+            a, b = early[10 + 2 * j + i], late[2 * j + i]
+            sums[10 + 4 * j + i] = jnp.where(h == 0, a, b)
+            sums[12 + 4 * j + i] = jnp.where(h == 0, b, a)
+    for n in range(10, 26):
+        gram[n:n + 1] = jnp.sum(sums[n], axis=0, keepdims=True)
+    reduce_start(local_total(), ra.at[0], r_send.at[0], r_recv.at[0], me1, peer1)
     halo_start(nf, 2, B)
-
-    def products(p, acc):
-        xs = [wide(xf, i, p) for i in range(NORB)]
-        ws = [wide(wf, i, p) for i in range(NORB)]
-        acc = list(acc)
-        for n, (i, j) in enumerate(PAIRS):
-            acc[n] = acc[n] + jnp.sum(xs[i] * xs[j], axis=0)
-        for j in range(NORB):
-            for i in range(NORB):
-                n = 10 + 4 * j + i
-                acc[n] = acc[n] + jnp.sum(xs[j] * ws[i], axis=0)
-        return tuple(acc)
-
-    zero = jnp.zeros((8, CO), jnp.float32)
-    acc = each_plane(products, (zero,) * 26)
-    reduce_start(local_sums(acc), ra.at[0], r_send.at[0], r_recv.at[0], me1, peer1)
 
     halo_finish(wf, 1, A)
     each(second, A)
@@ -372,10 +420,10 @@
     halo_finish(wf, 1, B)
     each(second, B)
     halo_start(mf, 3, B)
+    v = reduce_finish(ra.at[0], r_send.at[0], r_recv.at[0], peer1)
+    reduce_start(v, rb.at[0], r_send.at[1], r_recv.at[1], me2, peer2)
     halo_finish(nf, 2, A)
     each(smooth_x, A)
-    v = reduce_finish(ra.at[0], r_send.at[0], r_recv.at[0], peer1)
-    reduce_start(v, rb.at[0], r_send.at[1], r_recv.at[1], me2, peer2)
     halo_finish(nf, 2, B)
     each(smooth_x, B)
     halo_finish(mf, 3, A)
@@ -428,7 +476,7 @@
     for n, ij in enumerate(PAIRS):
         coef[n] = lowinv[ij]
 
-    def rotate(p, carry):
+    def rotate(p):
         ms = [narrow(base, j, p) for j in range(NORB)]
         for i in range(NORB):
             t = None
@@ -437,21 +485,22 @@
                     term = coef[n] * ms[j]
                     t = term if t is None else t + term
             new[i, p] = t.reshape(RW, CO)
-        return carry
-
-    each_plane(rotate)
 
     def back(j, i, m):
         hh, cc, pp = (h + j) % 2, (c + i) % 2, (x + m) % 2
         return new.at[2 * hh + cc, pl.ds(6 * pp, 6)], part(out_ref, x, h), b_send.at[4 * j + 2 * i + m], b_recv.at[2 * x + h], device(hh, cc, q, 2 * side + pp)
 
     order = [(j, i, m) for j in (1, 0) for i in (1, 0) for m in (1, 0)]
-    for jim in order:
-        a = back(*jim)
+    for m in (1, 0):
+        for p in range(6):
+            rotate(6 * ((x + m) % 2) + p)
+        for i in (1, 0):
+            remote(*back(1, i, m)).start()
+    for jim in order[4:]:
         if jim == (0, 0, 0):
-            local_or_remote(a)
+            local_or_remote(back(*jim))
         else:
-            remote(*a).start()
+            remote(*back(*jim)).start()
 
     unless_mine = jnp.logical_not(mine)
     for k in range(4):
@@ -499,12 +548,12 @@
         out_specs=pl.BlockSpec(memory_space=pltpu.VMEM),
         scratch_shapes=[
             vmem(*slab), pltpu.VMEM(slab, jnp.int32), pltpu.SMEM((NTYPES,), f32), pltpu.SMEM((NORB,), f32),
-            vmem(CO, CO), vmem(16, CO), vmem(16, CO),
+            pltpu.VMEM((2 * CO, 2 * CO), jnp.bfloat16), pltpu.VMEM((16, 2 * CO), jnp.bfloat16), pltpu.VMEM((32, 2 * CO), jnp.bfloat16),
             vmem(*wide), vmem(*wide), vmem(*wide), vmem(*wide),
             vmem(*slab), vmem(PL, RW, CO), vmem(*share), vmem(*share), vmem(*share),
             vmem(4, 2, rows, CO), vmem(4, 16, CO), vmem(2, 2, 16, CO),
-            vmem(4, 2, 16, rows), vmem(4, 2, 16, rows),
-            vmem(CO, CO), vmem(16, 8, CO), vmem(2, 16, 1, CO), vmem(2, 16, 1, CO),
+            vmem(4, 2, 3, 16, CO), vmem(4, 2, 3, 16, CO),
+            vmem(GRAM, CO), vmem(16, 8, CO), vmem(2, 16, 1, CO), vmem(2, 16, 1, CO),
             dma((4,)), dma((8,)), dma((8,)), dma((4,)), dma((4,)), dma((2,)), dma((2,)),
             dma((40,)), dma((40,)), dma((8,)), dma((8,)), dma((4,)), dma((4,)),
         ],

time: 71.1 us -> 66.9 us (0.941); the launches traced: 71 us -> 65.9 us
  Pallas kernels: 69.5 us -> 64.5 us
    pallas_call x1, Pallas kernels: 69.5 us -> 64.5 us  [body(): pl.pallas_call(kernel, out_shape=jax.ShapeDtypeStruct(slab, f32), in_spec...]
where the time goes in v3:
time: 66.9 us; the launch traced here: 65.9 us
  Pallas kernels  64.5 us (96%)
  local copies, waits for them, and re-layouts  1.42 us (2%)
    pallas_call x1, Pallas kernels, body(): pl.pallas_call(kernel, out_shape=jax.ShapeDtypeStruct(slab, f32), in_spec...  64.5 us
    unnamed x5, local copies, waits for them, and re-layouts  1.42 us

profile of v3, /device:TPU:64, one launch (start us, length us, event | category | flops | bytes accessed | tf_op | source)
XLA Modules:
  0.0 65.9 jit_solution(2588973093177182642)
XLA Ops:
  0.0 0.0 copy-start.1
  0.0 0.0 copy-start
  0.0 0.7 copy-done.1
  0.7 0.0 copy-done
  0.7 64.5 %step.1 = f32[6,64,256]{2,1,0:T(8,128)S(1)} custom-call(f32[6,64,256]{2,1,0:T(8,128)} %bitcast.3, s32[6,64,256]{2,1,0:T(8,128)} %type_hbm.1, f32[8]{0:T(128)S(1)} %copy-done, f32[4]{0:T(128)S(1)} %copy-done.1), custom_call_target="tpu_custom_call" | custom-call | tf_op jit(solution)/shard_map/step/pallas_call | solution.py:544
  65.2 0.7 %copy.6 = f32[1,6,64,256]{3,2,1,0:T(8,128)} copy(f32[1,6,64,256]{3,2,1,0:T(8,128)S(1)} %bitcast.2) | data formatting | bytes 786432
Async XLA Ops:
  0.0 0.7 copy-start.1
  0.0 0.7 %copy-start = (f32[8]{0:T(128)S(1)}, f32[8]{0:T(128)}, u32[]{:S(2)}) copy-start(f32[8]{0:T(128)} %table_hbm.1) | copy-start | bytes 100

commit v4 on v3

--- a/solution.py
+++ b/solution.py
@@ -26,6 +26,7 @@
 PL, RW, CO = 12, 16, 128
 H = 6
 GRAM = 32
+AHEAD = 3
 FAR_FIRST = (10, 6, 2, 14, 11, 7, 3, 15, 8, 9, 4, 12, 5, 13, 1)
 PAIRS = [(i, j) for i in range(NORB) for j in range(i + 1)]
 
@@ -97,6 +98,7 @@
     x_ref, type_ref, table_ref, step_ref, own_ref, pick_ref, spread_ref,
     xf, wf, nf, mf, vs, vf, base, vv, new, zz, zd_out, zd, zs, zr, gram, coef, ra, rb,
     in_sem, t_send, t_recv, d_send, d_recv, v_send, v_recv, h_send, h_recv, b_send, b_recv, r_send, r_recv,
+    e_send, e_recv, f_send, f_recv, eb,
 ):
     s = lax.axis_index("space")
     o = lax.axis_index("orb")
@@ -460,10 +462,20 @@
         return tuple(a + jnp.sum(ms[i] * ms[j], axis=0) for a, (i, j) in zip(acc, PAIRS))
 
     acc = each_plane(move, (zero,) * 10)
-    reduce_start(local_sums(acc), ra.at[1], r_send.at[2], r_recv.at[2], me1, peer1)
-    v = reduce_finish(ra.at[1], r_send.at[2], r_recv.at[2], peer1)
-    reduce_start(v, rb.at[1], r_send.at[3], r_recv.at[3], me2, peer2)
-    v = reduce_finish(rb.at[1], r_send.at[3], r_recv.at[3], peer2)
+    reduce_start(local_sums(acc), ra.at[1], r_send.at[2], r_recv.at[2], me2, peer2)
+
+    high = h == 1
+
+    def ahead(f, m):
+        pp = (x + m) % 2
+        return base.at[f, pl.ds(6 * pp, AHEAD)], eb.at[f, :, rows_of(x)], e_send.at[2 * f + m], e_recv.at[4 * f + x], device(1 - h, f % 2, q, 2 * side + pp)
+
+    for f in range(NORB):
+        for m in (1, 0):
+            guarded(None if f < 2 else jnp.logical_not(high), remote(*ahead(f, m)).start)
+    v = reduce_finish(ra.at[1], r_send.at[2], r_recv.at[2], peer2)
+    reduce_start(v, rb.at[1], r_send.at[3], r_recv.at[3], me1, peer1)
+    v = reduce_finish(rb.at[1], r_send.at[3], r_recv.at[3], peer1)
     low, inv = cholesky({(i, j): spread_out(v, n) for n, (i, j) in enumerate(PAIRS)})
     lowinv = {}
     for j in range(NORB):
@@ -488,20 +500,54 @@
 
     def back(j, i, m):
         hh, cc, pp = (h + j) % 2, (c + i) % 2, (x + m) % 2
-        return new.at[2 * hh + cc, pl.ds(6 * pp, 6)], part(out_ref, x, h), b_send.at[4 * j + 2 * i + m], b_recv.at[2 * x + h], device(hh, cc, q, 2 * side + pp)
+        n = 4 * j + 2 * i + m
+        src, dst = new.at[2 * hh + cc, pl.ds(6 * pp + AHEAD * j, 6 - AHEAD * j)], part(out_ref, x, h).at[pl.ds(AHEAD * j, 6 - AHEAD * j)]
+        return src, dst, b_send.at[n], b_recv.at[2 * x + h], device(hh, cc, q, 2 * side + pp)
 
     order = [(j, i, m) for j in (1, 0) for i in (1, 0) for m in (1, 0)]
     for m in (1, 0):
-        for p in range(6):
+        for p in range(AHEAD, 6):
             rotate(6 * ((x + m) % 2) + p)
         for i in (1, 0):
             remote(*back(1, i, m)).start()
+    for p in range(AHEAD):
+        rotate(p)
+        rotate(6 + p)
     for jim in order[4:]:
         if jim == (0, 0, 0):
             local_or_remote(back(*jim))
         else:
             remote(*back(*jim)).start()
 
+    def came(f):
+        for xx in range(4):
+            ref = eb.at[f, :, pl.ds(16 * xx, 16)]
+            remote(ref, ref, e_send.at[0], e_recv.at[4 * f + xx], across).wait_recv()
+
+    def pass_on(f):
+        return remote(eb.at[f], eb.at[f], f_send.at[f], f_recv.at[f], device(h, 1 - c, q, x))
+
+    gives = {0: c == 0, 1: jnp.logical_and(c == 1, high), 2: jnp.logical_and(c == 0, high)}
+    takes = {0: c == 1, 1: jnp.logical_and(c == 0, high), 2: jnp.logical_and(c == 1, high)}
+    for f in range(NORB):
+        @pl.when(jnp.logical_and(c == f % 2, high) if f > 1 else c == f % 2)
+        def _():
+            came(f)
+
+        if f < 3:
+            guarded(gives[f], pass_on(f).start)
+    for f in range(3):
+        guarded(takes[f], pass_on(f).wait_recv)
+    for i in range(NORB):
+        @pl.when(o == i)
+        def _():
+            t = None
+            for n, (a, j) in enumerate(PAIRS):
+                if a == i:
+                    term = coef[n] * eb[j].reshape(8 * AHEAD, 8, CO)
+                    t = term if t is None else t + term
+            out_ref[0:AHEAD, :, cols_of(1 - h)] = t.reshape(AHEAD, 64, CO)
+
     unless_mine = jnp.logical_not(mine)
     for k in range(4):
         remote(*scatter(1, k)).wait_send()
@@ -522,10 +568,16 @@
         halo_sent(f, r, B, r > 0)
     for jim in order:
         guarded(unless_mine if jim == (0, 0, 0) else None, remote(*back(*jim)).wait_send)
+    for f in range(NORB):
+        for m in (1, 0):
+            guarded(None if f < 2 else jnp.logical_not(high), remote(*ahead(f, m)).wait_send)
+    for f in range(3):
+        guarded(gives[f], pass_on(f).wait_send)
     for xx in range(4):
-        for hh in range(2):
-            dst = out_ref.at[:, pl.ds(16 * xx, 16), pl.ds(CO * hh, CO)]
-            remote(dst, dst, b_send.at[0], b_recv.at[2 * xx + hh], across).wait_recv()
+        dst = part(out_ref, xx, h)
+        remote(dst, dst, b_send.at[0], b_recv.at[2 * xx + h], across).wait_recv()
+        dst = part(out_ref, xx, 1 - h).at[pl.ds(AHEAD, 6 - AHEAD)]
+        remote(dst, dst, b_send.at[0], b_recv.at[2 * xx + 1 - h], across).wait_recv()
 
 
 def body(orbitals, atom_type, type_table, step_length):
@@ -556,6 +608,7 @@
             vmem(GRAM, CO), vmem(16, 8, CO), vmem(2, 16, 1, CO), vmem(2, 16, 1, CO),
             dma((4,)), dma((8,)), dma((8,)), dma((4,)), dma((4,)), dma((2,)), dma((2,)),
             dma((40,)), dma((40,)), dma((8,)), dma((8,)), dma((4,)), dma((4,)),
+            dma((8,)), dma((16,)), dma((3,)), dma((3,)), vmem(NORB, AHEAD, 64, CO),
         ],
         compiler_params=pltpu.CompilerParams(
             collective_id=0, has_side_effects=True, vmem_limit_bytes=55993958

time: 66.9 us -> 65.6 us (0.981)
  the two profiles are of different devices: /device:TPU:64 before, /device:TPU:32 now
where the time goes in v4:
time: 65.6 us; the launch traced here: 65.5 us
  Pallas kernels  64.1 us (98%)
  local copies, waits for them, and re-layouts  1.42 us (2%)
    pallas_call x1, Pallas kernels, body(): pl.pallas_call(kernel, out_shape=jax.ShapeDtypeStruct(slab, f32), in_spec...  64.1 us
    unnamed x5, local copies, waits for them, and re-layouts  1.42 us

profile of v4, /device:TPU:32, one launch (start us, length us, event | category | flops | bytes accessed | tf_op | source)
XLA Modules:
  0.0 65.5 jit_solution(9678399537635312504)
XLA Ops:
  0.0 0.0 copy-start.1
  0.0 0.0 copy-start
  0.0 0.7 copy-done.1
  0.7 0.0 copy-done
  0.7 64.1 %step.1 = f32[6,64,256]{2,1,0:T(8,128)S(1)} custom-call(f32[6,64,256]{2,1,0:T(8,128)} %bitcast.3, s32[6,64,256]{2,1,0:T(8,128)} %type_hbm.1, f32[8]{0:T(128)S(1)} %copy-done, f32[4]{0:T(128)S(1)} %copy-done.1), custom_call_target="tpu_custom_call" | custom-call | tf_op jit(solution)/shard_map/step/pallas_call | solution.py:596
  64.8 0.7 %copy.6 = f32[1,6,64,256]{3,2,1,0:T(8,128)} copy(f32[1,6,64,256]{3,2,1,0:T(8,128)S(1)} %bitcast.2) | data formatting | bytes 786432
Async XLA Ops:
  0.0 0.7 %copy-start.1 = (f32[4]{0:T(128)S(1)}, f32[4]{0:T(128)}, u32[]{:S(2)}) copy-start(f32[4]{0:T(128)} %step_hbm.1) | copy-start | bytes 52
  0.0 0.7 %copy-start = (f32[8]{0:T(128)S(1)}, f32[8]{0:T(128)}, u32[]{:S(2)}) copy-start(f32[8]{0:T(128)} %table_hbm.1) | copy-start | bytes 100

commit v5 on v4

--- a/solution.py
+++ b/solution.py
@@ -361,11 +361,8 @@
         i = 2 * pair + i
         vv[i, p] = P1 * xf[i, p + H, 8:8 + RW] + (P2 + SHIFT * P3) * nf[i, p + H, 8:8 + RW] + P3 * k
 
-    def smooth_w(pair, i, p):
-        k = taps_xy(mf, 3, pair, i, p)
-        i = 2 * pair + i
-        t = P1 * wf[i, p + H, 8:8 + RW] + (P2 + SHIFT * P3) * mf[i, p + H, 8:8 + RW] + P3 * k
-        base[i, p] = xf[i, p + H, 8:8 + RW] - step_ref[i] * t
+    def keep_taps(pair, i, p):
+        zz[3, pair, pl.ds(pl.multiple_of((i * PL + p) * RW, RW), RW)] = taps_xy(mf, 3, pair, i, p)
 
     def arrived(pair):
         for i in range(2):
@@ -416,12 +413,12 @@
     reduce_start(local_total(), ra.at[0], r_send.at[0], r_recv.at[0], me1, peer1)
     halo_start(nf, 2, B)
 
+    halo_finish(wf, 1, B)
+    each(second, B)
+    halo_start(mf, 3, B)
     halo_finish(wf, 1, A)
     each(second, A)
     halo_start(mf, 3, A)
-    halo_finish(wf, 1, B)
-    each(second, B)
-    halo_start(mf, 3, B)
     v = reduce_finish(ra.at[0], r_send.at[0], r_recv.at[0], peer1)
     reduce_start(v, rb.at[0], r_send.at[1], r_recv.at[1], me2, peer2)
     halo_finish(nf, 2, A)
@@ -429,10 +426,7 @@
     halo_finish(nf, 2, B)
     each(smooth_x, B)
     halo_finish(mf, 3, A)
-    each(smooth_w, A)
-    halo_finish(mf, 3, B)
-    each(smooth_w, B)
-
+    each(keep_taps, A)
     v = reduce_finish(rb.at[0], r_send.at[1], r_recv.at[1], peer2)
     margin = {(i, j): spread_out(v, n) for n, (i, j) in enumerate(PAIRS)}
     low, inv = cholesky(margin)
@@ -450,18 +444,32 @@
             y[j] = t * inv[j]
             coef[4 * i + j] = step_ref[i] * y[j]
 
+    def prepare(p, carry):
+        vs4 = [narrow(vv, j, p) for j in range(NORB)]
+        for pair in (A, B):
+            for n in range(2):
+                i = 2 * pair + n
+                t = P1 * wide(wf, i, p) + (P2 + SHIFT * P3) * wide(mf, i, p)
+                if pair is A:
+                    at = pl.ds(pl.multiple_of((n * PL + p) * RW, RW), RW)
+                    t = t + P3 * zz[3, A, at].reshape(2, 8, CO)
+                t = wide(xf, i, p) - step_ref[i] * t
+                for j in range(NORB):
+                    t = t + coef[4 * i + j] * vs4[j]
+                base[i, p] = t.reshape(RW, CO)
+        return carry
+
+    each_plane(prepare)
+    halo_finish(mf, 3, B)
+
     def move(p, acc):
-        vs4 = [narrow(vv, j, p) for j in range(NORB)]
-        ms = []
-        for i in range(NORB):
-            t = narrow(base, i, p)
-            for j in range(NORB):
-                t = t + coef[4 * i + j] * vs4[j]
-            base[i, p] = t.reshape(RW, CO)
-            ms.append(t)
+        for n in range(2):
+            i = 2 * B + n
+            base[i, p] = base[i, p] - (P3 * step_ref[i]) * taps_xy(mf, 3, B, n, p)
+        ms = [narrow(base, i, p) for i in range(NORB)]
         return tuple(a + jnp.sum(ms[i] * ms[j], axis=0) for a, (i, j) in zip(acc, PAIRS))
 
-    acc = each_plane(move, (zero,) * 10)
+    acc = each_plane(move, (jnp.zeros((8, CO), jnp.float32),) * 10)
     reduce_start(local_sums(acc), ra.at[1], r_send.at[2], r_recv.at[2], me2, peer2)
 
     high = h == 1
@@ -470,11 +478,17 @@
         pp = (x + m) % 2
         return base.at[f, pl.ds(6 * pp, AHEAD)], eb.at[f, :, rows_of(x)], e_send.at[2 * f + m], e_recv.at[4 * f + x], device(1 - h, f % 2, q, 2 * side + pp)
 
-    for f in range(NORB):
+    for f in (0, 1, 2):
         for m in (1, 0):
-            guarded(None if f < 2 else jnp.logical_not(high), remote(*ahead(f, m)).start)
+            guarded(jnp.logical_not(high), remote(*ahead(f, m)).start)
     v = reduce_finish(ra.at[1], r_send.at[2], r_recv.at[2], peer2)
     reduce_start(v, rb.at[1], r_send.at[3], r_recv.at[3], me1, peer1)
+    for f in (3,):
+        for m in (1, 0):
+            guarded(jnp.logical_not(high), remote(*ahead(f, m)).start)
+    for f in (0, 1):
+        for m in (1, 0):
+            guarded(high, remote(*ahead(f, m)).start)
     v = reduce_finish(rb.at[1], r_send.at[3], r_recv.at[3], peer1)
     low, inv = cholesky({(i, j): spread_out(v, n) for n, (i, j) in enumerate(PAIRS)})
     lowinv = {}

time: 65.6 us -> 64.1 us (0.977)
  the two profiles are of different devices: /device:TPU:32 before, /device:TPU:64 now
where the time goes in v5:
time: 64.1 us; the launch traced here: 63.5 us
  Pallas kernels  62.1 us (97%)
  local copies, waits for them, and re-layouts  1.42 us (2%)
    pallas_call x1, Pallas kernels, body(): pl.pallas_call(kernel, out_shape=jax.ShapeDtypeStruct(slab, f32), in_spec...  62.1 us
    unnamed x5, local copies, waits for them, and re-layouts  1.42 us

profile of v5, /device:TPU:64, one launch (start us, length us, event | category | flops | bytes accessed | tf_op | source)
XLA Modules:
  0.0 63.5 jit_solution(6712154518211658636)
XLA Ops:
  0.0 0.0 copy-start.1
  0.0 0.0 copy-start
  0.0 0.7 %copy-done.1 = f32[4]{0:T(128)S(1)} copy-done((f32[4]{0:T(128)S(1)}, f32[4]{0:T(128)}, u32[]{:S(2)}) %copy-start.1) | copy-done | bytes 40
  0.7 0.0 copy-done
  0.7 62.1 %step.1 = f32[6,64,256]{2,1,0:T(8,128)S(1)} custom-call(f32[6,64,256]{2,1,0:T(8,128)} %bitcast.3, s32[6,64,256]{2,1,0:T(8,128)} %type_hbm.1, f32[8]{0:T(128)S(1)} %copy-done, f32[4]{0:T(128)S(1)} %copy-done.1), custom_call_target="tpu_custom_call" | custom-call | tf_op jit(solution)/shard_map/step/pallas_call | solution.py:610
  62.8 0.7 %copy.6 = f32[1,6,64,256]{3,2,1,0:T(8,128)} copy(f32[1,6,64,256]{3,2,1,0:T(8,128)S(1)} %bitcast.2) | data formatting | bytes 786432
Async XLA Ops:
  0.0 0.7 %copy-start.1 = (f32[4]{0:T(128)S(1)}, f32[4]{0:T(128)}, u32[]{:S(2)}) copy-start(f32[4]{0:T(128)} %step_hbm.1) | copy-start | bytes 52
  0.0 0.7 %copy-start = (f32[8]{0:T(128)S(1)}, f32[8]{0:T(128)}, u32[]{:S(2)}) copy-start(f32[8]{0:T(128)} %table_hbm.1) | copy-start | bytes 100

commit v6 on v5

--- a/solution.py
+++ b/solution.py
@@ -262,14 +262,17 @@
 
     def halo_start(f, r, pair, with_z=True):
         copies = halo_copies(f, r, pair)
+        if not with_z:
+            for n in (0, 1, 2, 3):
+                guarded(copies[n][0], copies[n][1].start)
         flat = joined(share(f, pair), 1)
         if with_z:
             edge = dot16(pick_ref[...], flat, 1, 1)
             for b in range(3):
                 zs[r, pair, b] = edge[:, CO * b:CO * b + CO]
             copies[4][1].start()
-        for n in (0, 1, 2, 3):
-            guarded(copies[n][0], copies[n][1].start)
+            for n in (0, 1, 2, 3):
+                guarded(copies[n][0], copies[n][1].start)
         zz[r, pair] = both(dot16(flat, own_ref[...], 1, 0))
 
     def halo_finish(f, r, pair, with_z=True):

time: 64.1 us -> 64 us (level)
  no operation moved by 1% of the time
where the time goes in v6:
time: 64 us; the launch traced here: 63.5 us
  Pallas kernels  62 us (97%)
  local copies, waits for them, and re-layouts  1.42 us (2%)
    pallas_call x1, Pallas kernels, body(): pl.pallas_call(kernel, out_shape=jax.ShapeDtypeStruct(slab, f32), in_spec...  62 us
    unnamed x5, local copies, waits for them, and re-layouts  1.42 us

profile of v6, /device:TPU:64, one launch (start us, length us, event | category | flops | bytes accessed | tf_op | source)
XLA Modules:
  0.0 63.5 jit_solution(14997812793919145499)
XLA Ops:
  0.0 0.0 copy-start.1
  0.0 0.0 copy-start
  0.0 0.7 %copy-done.1 = f32[4]{0:T(128)S(1)} copy-done((f32[4]{0:T(128)S(1)}, f32[4]{0:T(128)}, u32[]{:S(2)}) %copy-start.1) | copy-done | bytes 40
  0.7 0.0 copy-done
  0.7 62.0 %step.1 = f32[6,64,256]{2,1,0:T(8,128)S(1)} custom-call(f32[6,64,256]{2,1,0:T(8,128)} %bitcast.3, s32[6,64,256]{2,1,0:T(8,128)} %type_hbm.1, f32[8]{0:T(128)S(1)} %copy-done, f32[4]{0:T(128)S(1)} %copy-done.1), custom_call_target="tpu_custom_call" | custom-call | tf_op jit(solution)/shard_map/step/pallas_call | solution.py:613
  62.7 0.7 %copy.6 = f32[1,6,64,256]{3,2,1,0:T(8,128)} copy(f32[1,6,64,256]{3,2,1,0:T(8,128)S(1)} %bitcast.2) | data formatting | bytes 786432
Async XLA Ops:
  0.0 0.7 %copy-start.1 = (f32[4]{0:T(128)S(1)}, f32[4]{0:T(128)}, u32[]{:S(2)}) copy-start(f32[4]{0:T(128)} %step_hbm.1) | copy-start | bytes 52
  0.0 0.7 %copy-start = (f32[8]{0:T(128)S(1)}, f32[8]{0:T(128)}, u32[]{:S(2)}) copy-start(f32[8]{0:T(128)} %table_hbm.1) | copy-start | bytes 100
